TPU v7x, 32 devices: a whole 2x2x4 slice. The times are simulated.
32 devices in a mesh: dp: 2 (over y), member: 4 (over z), mp: 4 (over x, core).
Axes of the slice: x: 2, y: 2, z: 4, core: 2. Of those that a mesh axis runs over, the one named last changes fastest.
Arguments:
- hidden: bfloat16 [256, 4096], P('dp', ('member', 'mp')), may hold values from -9 to 9
- w_in: bfloat16 [4, 4096, 4096], P('member', 'dp', 'mp'), may hold values from -0.09375 to 0.09375
- w_out: bfloat16 [4, 4096, 4096], P('member', 'mp', 'dp'), may hold values from -0.09375 to 0.09375
- score_vec: float32 [4, 4096], P('member'), may hold values from -1 to 1
- lengths: int32 [2, 4], P('dp'), may hold values from 1 to 64, 128 in all within a row
- reward_offset: int32 [2, 4], P('dp'), may hold values from 0 to 63
- seq_weight: float32 [2, 4], P('dp'), may hold values from -4 to 4
Outputs:
- penalized: float32 [2, 4], P('dp')
- grad_hidden: float32 [256, 4096], P('dp', ('member', 'mp'))
- grad_in: float32 [4, 4096, 4096], P('member', 'dp', 'mp')
- grad_out: float32 [4, 4096, 4096], P('member', 'mp', 'dp')
Inputs may be any that keep to these rules, and one draw needn't show every extreme that they name: Each row of lengths sums to 128, and its largest entry is exactly 64.
All inputs are finite; a program needn't handle non-finite values.
Results may differ from a plain program's by a relative error of at most 0.018.
Values may be sent and summed in bfloat16 or wider, within the bound.
A program may use at most 64 MiB of HBM per device.

v0:
```python
import jax
import jax.numpy as jnp
from jax import lax
from jax.sharding import PartitionSpec as P

PENALTY = 0.5
SPREAD_FLOOR = 0.25
EPSILON = 1e-05
PRECISE = lax.Precision.HIGHEST
AGAINST = (((1,), (1,)), ((), ()))


def pooling(lengths, offsets, row_count):
    seq_ends = jnp.cumsum(lengths)
    seq_starts = seq_ends - lengths
    target = seq_starts + offsets % lengths
    places = jnp.arange(row_count, dtype=jnp.int32)[:, None]
    inside = jnp.logical_and(places >= seq_starts[None, :], places < seq_ends[None, :])
    marked = places == target[None, :]
    return inside.astype(jnp.float32) / lengths.astype(jnp.float32)[None, :] + marked.astype(
        jnp.float32
    )


def silu_slope(gate_in):
    sigmoided = jax.nn.sigmoid(gate_in)
    return sigmoided * (1.0 + gate_in * (1.0 - sigmoided))


def slab_terms(left, right, slab_count):
    left_blocks = left.reshape(slab_count, left.shape[0] // slab_count, left.shape[1])
    right_blocks = right.reshape(slab_count, right.shape[0] // slab_count, right.shape[1])
    terms = jnp.einsum(
        "bsd,bsf->bdf", left_blocks, right_blocks, preferred_element_type=jnp.float32
    )
    rounded = lax.optimization_barrier(terms.astype(jnp.bfloat16))
    return jnp.sum(rounded.astype(jnp.float32), axis=0)


def local(hidden, w_in, w_out, score_vec, lengths, reward_offset, seq_weight):
    members = lax.axis_size("member")
    trunk_rows = lax.all_gather(hidden, ("member", "mp"), axis=1, tiled=True)
    w_first = w_in[0]
    w_second = w_out[0]
    vector = score_vec[0]
    feature_count = trunk_rows.shape[1]
    row_count = trunk_rows.shape[0]
    pooler = pooling(lengths[0], reward_offset[0], row_count)
    slab_count = lax.axis_size("dp")
    slab_cols = lax.all_to_all(trunk_rows, "dp", split_axis=1, concat_axis=0, tiled=True)
    rows_here = slab_cols
    gate_in = lax.psum_scatter(
        jnp.dot(rows_here, w_first, preferred_element_type=jnp.float32).astype(jnp.bfloat16),
        "dp",
        scatter_dimension=0,
        tiled=True,
    ).astype(jnp.float32)
    activated = jax.nn.silu(gate_in).astype(jnp.bfloat16)
    act_every = lax.all_gather(activated, "dp", axis=0, tiled=True)
    branch_cols = jnp.dot(act_every, w_second, preferred_element_type=jnp.float32)
    branch = lax.all_to_all(
        branch_cols.astype(jnp.bfloat16), "dp", split_axis=0, concat_axis=1, tiled=True
    ).astype(branch_cols.dtype)
    combined = trunk_rows.astype(jnp.float32) + lax.psum(branch.astype(jnp.bfloat16), "mp").astype(
        jnp.float32
    )
    inverse = lax.rsqrt(jnp.mean(combined * combined, axis=1) + EPSILON)
    scores = jnp.dot(combined, vector, precision=PRECISE) * inverse
    rewards = jnp.dot(scores, pooler, precision=PRECISE)
    center = lax.psum(rewards, "member") / members
    spread = lax.psum((rewards - center) ** 2, "member") / members
    deviation = jnp.sqrt(spread + SPREAD_FLOOR)
    penalized = center - PENALTY * deviation
    seq_pull = seq_weight[0] * (1.0 - PENALTY * (rewards - center) / deviation) / members
    tok_weight = jnp.dot(pooler, seq_pull, precision=PRECISE)
    slopes = tok_weight[:, None] * (
        vector[None, :] * inverse[:, None]
        - (scores * inverse * inverse / feature_count)[:, None] * combined
    )
    slope_half = slopes.astype(jnp.bfloat16)
    direct = slopes * (lax.axis_index("mp") == 0).astype(jnp.float32)
    slope_every = lax.all_to_all(slope_half, "dp", split_axis=1, concat_axis=0, tiled=True)
    rows_here = slope_every
    back_raw = lax.psum_scatter(
        lax.dot_general(rows_here, w_second, AGAINST, preferred_element_type=jnp.float32).astype(
            jnp.bfloat16
        ),
        "dp",
        scatter_dimension=0,
        tiled=True,
    ).astype(jnp.float32)
    back_gate = (back_raw * silu_slope(gate_in)).astype(jnp.bfloat16)
    gate_every = lax.all_gather(back_gate, "dp", axis=0, tiled=True)
    back_cols = lax.dot_general(gate_every, w_first, AGAINST, preferred_element_type=jnp.float32)
    hidden_term = direct + lax.all_to_all(
        back_cols.astype(jnp.bfloat16), "dp", split_axis=0, concat_axis=1, tiled=True
    ).astype(back_cols.dtype)
    grad_in = slab_terms(slab_cols, gate_every, slab_count)
    grad_out = slab_terms(act_every, slope_every, slab_count)
    grad_hidden = lax.psum_scatter(
        hidden_term.astype(jnp.bfloat16), ("member", "mp"), scatter_dimension=1, tiled=True
    ).astype(jnp.float32)
    return (penalized[None, :], grad_hidden, grad_in[None], grad_out[None])


def solution(mesh):
    in_specs = (
        P("dp", ("member", "mp")),
        P("member", "dp", "mp"),
        P("member", "mp", "dp"),
        P("member", None),
        P("dp", None),
        P("dp", None),
        P("dp", None),
    )
    out_specs = (
        P("dp", None),
        P("dp", ("member", "mp")),
        P("member", "dp", "mp"),
        P("member", "mp", "dp"),
    )
    return jax.shard_map(local, mesh=mesh, in_specs=in_specs, out_specs=out_specs, check_vma=False)
```

profile of v0, /device:TPU:13, one launch (start us, length us, event | category | flops | bytes accessed | tf_op | source)
XLA Modules:
  0.0 315.2 jit_solution(12053191525495142274)
XLA Ops:
  8.9 40.4 %all-gather.2.cloned.1.call-done = bf16[128,4096]{0,1:T(8,128)(2,1)} async-done(((bf16[128,256]{0,1:T(8,128)(2,1)}), bf16[128,4096]{0,1:T(8,128)(2,1)}) %all-gather.2.cloned.1.call-update) | async-done | bytes 1048592 | tf_op jit(solution)/shard_map/all_gather | solution.py:42
  50.8 15.0 %all_to_all.70 = bf16[128,2,2048]{2,0,1:T(8,128)(2,1)S(1)} all-to-all(bf16[128,2,2048]{2,0,1:T(8,128)(2,1)S(1)} %copy.33), channel_id=1, replica_groups=mesh['dp'=2,'member'=4,'mp'=4] {'dp'}, dimensions={1} | all-to-all | bytes 2097152 | tf_op jit(solution)/shard_map/all_to_all | solution.py:50
  65.8 4.2 %fusion.17 = bf16[256,1024]{1,0:T(8,128)(2,1)} fusion(bf16[256,2048]{1,0:T(8,128)(2,1)S(1)} %bitcast.98, bf16[1,2048,1024]{2,1,0:T(8,128)(2,1)} %param.8), kind=kOutput, calls=%fused_computation.22 | convolution fusion | flops 1074003968 | bytes 5767168 | tf_op jit(solution)/shard_map/dot_general | solution.py:53
  70.1 14.0 %reduce-scatter.4.cloned.1.call-done = bf16[128,1024]{1,0:T(8,128)(2,1)} async-done(((bf16[256,1024]{1,0:T(8,128)(2,1)}), bf16[128,1024]{1,0:T(8,128)(2,1)}) %reduce-scatter.4.cloned.1.call-update) | async-done | bytes 262160 | tf_op jit(solution)/shard_map/reduce_scatter | solution.py:52
  85.2 7.9 %all_gather.10 = bf16[256,1024]{1,0:T(8,128)(2,1)S(1)} all-gather(bf16[128,1024]{1,0:T(8,128)(2,1)S(1)} %fusion.30), channel_id=1, replica_groups=mesh['dp'=2,'member'=4,'mp'=4] {'dp'}, dimensions={0}, use_global_device_ids=true | all-gather | bytes 786432 | tf_op jit(solution)/shard_map/all_gather | solution.py:59
  93.1 3.6 %fusion.11 = bf16[256,2048]{1,0:T(8,128)(2,1)S(1)} fusion(bf16[256,1024]{1,0:T(8,128)(2,1)S(1)} %all_gather.10, bf16[1,1024,2048]{2,1,0:T(8,128)(2,1)} %param.9), kind=kOutput, calls=%fused_computation.13 | convolution fusion | flops 1074266112 | bytes 5767168 | tf_op jit(solution)/shard_map/dot_general | solution.py:60
  96.8 14.5 %all_to_all.71 = bf16[2,128,2048]{2,1,0:T(8,128)(2,1)S(1)} all-to-all(bf16[2,128,2048]{2,1,0:T(8,128)(2,1)S(1)} %bitcast.106), channel_id=1, replica_groups=mesh['dp'=2,'member'=4,'mp'=4] {'dp'}, dimensions={0} | all-to-all | bytes 2097152 | tf_op jit(solution)/shard_map/all_to_all | solution.py:61
  113.0 38.1 %all-reduce.2.cloned.1.call-done = bf16[128,4096]{0,1:T(8,128)(2,1)} async-done(((bf16[128,4096]{0,1:T(8,128)(2,1)}), bf16[128,4096]{0,1:T(8,128)(2,1)}) %all-reduce.2.cloned.1.call-update) | async-done | bytes 1048592 | tf_op jit(solution)/shard_map/psum | solution.py:64
  154.6 6.9 %psum.22 = f32[4]{0:T(128)S(1)} all-reduce(f32[4]{0:T(128)S(1)} %convolution_bitcast_fusion.1), channel_id=1, replica_groups=mesh['dp'=2,'member'=4,'mp'=4] {'member'}, use_global_device_ids=true, to_apply=%region_4.5 | all-reduce | flops 4 | bytes 32 | tf_op jit(solution)/shard_map/psum | solution.py:70
  161.4 9.6 %psum.23 = f32[4]{0:T(128)S(1)} all-reduce(f32[4]{0:T(128)S(1)} %fusion.52), channel_id=1, replica_groups=mesh['dp'=2,'member'=4,'mp'=4] {'member'}, use_global_device_ids=true, to_apply=%region_5.6 | all-reduce | flops 4 | bytes 32 | tf_op jit(solution)/shard_map/psum | solution.py:71
  175.0 11.1 %all_to_all.72 = bf16[128,2,2048]{2,0,1:T(8,128)(2,1)S(1)} all-to-all(bf16[128,2,2048]{2,0,1:T(8,128)(2,1)} %copy.35), channel_id=1, replica_groups=mesh['dp'=2,'member'=4,'mp'=4] {'dp'}, dimensions={1} | all-to-all | bytes 2097152 | tf_op jit(solution)/shard_map/all_to_all | solution.py:82
  187.1 4.4 %fusion.20 = bf16[256,1024]{1,0:T(8,128)(2,1)} fusion(bf16[256,2048]{1,0:T(8,128)(2,1)S(1)} %bitcast.99, bf16[1,1024,2048]{2,1,0:T(8,128)(2,1)} %param.9), kind=kOutput, calls=%fused_computation.23 | convolution fusion | flops 1074003968 | bytes 5767168 | tf_op jit(solution)/shard_map/dot_general | solution.py:85
  191.6 18.4 %reduce-scatter.6.cloned.1.call-done = bf16[128,1024]{1,0:T(8,128)(2,1)} async-done(((bf16[256,1024]{1,0:T(8,128)(2,1)}), bf16[128,1024]{1,0:T(8,128)(2,1)}) %reduce-scatter.6.cloned.1.call-update) | async-done | bytes 262160 | tf_op jit(solution)/shard_map/reduce_scatter | solution.py:84
  211.2 7.9 %all_gather.11 = bf16[256,1024]{1,0:T(8,128)(2,1)S(1)} all-gather(bf16[128,1024]{1,0:T(8,128)(2,1)S(1)} %fusion.34), channel_id=1, replica_groups=mesh['dp'=2,'member'=4,'mp'=4] {'dp'}, dimensions={0}, use_global_device_ids=true | all-gather | bytes 786432 | tf_op jit(solution)/shard_map/all_gather | solution.py:93
  219.0 4.6 %fusion.8 = bf16[256,2048]{1,0:T(8,128)(2,1)} fusion(bf16[256,1024]{1,0:T(8,128)(2,1)S(1)} %all_gather.11, bf16[1,2048,1024]{2,1,0:T(8,128)(2,1)} %param.8), kind=kOutput, calls=%fused_computation.12 | convolution fusion | flops 1074266112 | bytes 5767168 | tf_op jit(solution)/shard_map/dot_general | solution.py:94
  223.6 5.6 %all-to-all-start.3 = ((bf16[2,128,2048]{2,1,0:T(8,128)(2,1)}), bf16[2,128,2048]{2,1,0:T(8,128)(2,1)}, u32[]{:S(2)}, u32[]{:S(2)}) async-start(bf16[2,128,2048]{2,1,0:T(8,128)(2,1)} %bitcast.105), calls=%async_computation.5 | async-start | bytes 2097152 | tf_op jit(solution)/shard_map/all_to_all | solution.py:95
  229.8 10.5 %all-to-all-done.3 = bf16[2,128,2048]{2,1,0:T(8,128)(2,1)} async-done(((bf16[2,128,2048]{2,1,0:T(8,128)(2,1)}), bf16[2,128,2048]{2,1,0:T(8,128)(2,1)}, u32[]{:S(2)}, u32[]{:S(2)}) %all-to-all-start.3) | async-done | bytes 1048608 | tf_op jit(solution)/shard_map/all_to_all | solution.py:95
  243.1 2.9 copy.36
  248.8 7.2 %convolution_convert_fusion = bf16[2,1024,2048]{2,1,0:T(8,128)(2,1)} fusion(bf16[2,128,1024]{2,1,0:T(8,128)(2,1)} %bitcast.103, bf16[128,2,2048]{2,0,1:T(8,128)(2,1)} %copy-done.2), kind=kOutput, calls=%fused_computation.3 | convolution fusion | flops 1077936128 | bytes 9961472 | tf_op jit(solution)/shard_map/bsd,bsf->bdf/dot_general | solution.py:33
  256.0 9.9 %convert_reduce_fusion = f32[1024,2048]{1,0:T(8,128)} fusion(bf16[2,1024,2048]{2,1,0:T(8,128)(2,1)} %convolution_convert_fusion), kind=kLoop, calls=%fused_computation | loop fusion | flops 6291456 | bytes 16777216 | tf_op jit(solution)/shard_map/reduce_sum | solution.py:37
  265.8 5.8 %convert_bitcast_fusion = bf16[2,2048,1024]{1,2,0:T(8,128)(2,1)} fusion(bf16[2,128,1024]{2,1,0:T(8,128)(2,1)S(1)} %bitcast.104, bf16[128,2,2048]{2,0,1:T(8,128)(2,1)S(1)} %all_to_all.70), kind=kOutput, calls=%fused_computation.2 | convolution fusion | flops 1077936128 | bytes 9961472 | tf_op jit(solution)/shard_map/bsd,bsf->bdf/dot_general | solution.py:33
  271.6 9.6 %convert_reduce_fusion.1 = f32[2048,1024]{0,1:T(8,128)} fusion(bf16[2,2048,1024]{1,2,0:T(8,128)(2,1)} %convert_bitcast_fusion), kind=kLoop, calls=%fused_computation.1 | loop fusion | flops 6291456 | bytes 16777216 | tf_op jit(solution)/shard_map/reduce_sum | solution.py:37
  281.2 9.3 %copy.40 = f32[1,2048,1024]{2,1,0:T(8,128)} copy(f32[1,2048,1024]{1,2,0:T(8,128)} %bitcast.95) | data formatting | bytes 16777216
  290.5 16.6 %reduce-scatter.8.cloned.1.call-done = bf16[128,256]{0,1:T(8,128)(2,1)} async-done(((bf16[128,4096]{0,1:T(8,128)(2,1)}), bf16[128,256]{0,1:T(8,128)(2,1)}) %reduce-scatter.8.cloned.1.call-update) | async-done | bytes 65552 | tf_op jit(solution)/shard_map/reduce_scatter | solution.py:100
  (50 shorter events, 23.4 us)
Async XLA Ops:
  7.2 42.1 %all-gather.2.cloned.1.call-start = ((), (), s32[]{:S(2)}) async-start(), calls=%async_computation.7 | async-start | bytes 1114112 | tf_op jit(solution)/shard_map/all_gather | solution.py:42
  8.8 75.3 %reduce-scatter.4.cloned.1.call-start = ((), (), s32[]{:S(2)}) async-start(), calls=%async_computation.8 | async-start | bytes 786432 | tf_op jit(solution)/shard_map/reduce_scatter | solution.py:52
  70.0 81.1 %all-reduce.2.cloned.1.call-start = ((), (), s32[]{:S(2)}) async-start(), calls=%async_computation.9 | async-start | bytes 2097152 | tf_op jit(solution)/shard_map/psum | solution.py:64
  93.1 3.7 %copy-start.3 = (bf16[256,1024]{1,0:T(8,128)(2,1)}, bf16[256,1024]{1,0:T(8,128)(2,1)S(1)}, u32[]{:S(2)}) copy-start(bf16[256,1024]{1,0:T(8,128)(2,1)S(1)} %all_gather.10) | copy-start | bytes 1572868
  111.3 1.4 copy-start.8
  111.3 1.6 copy-start.9
  111.3 39.8 %copy-start = (bf16[128,4096]{0,1:T(8,128)(2,1)S(1)}, bf16[128,4096]{0,1:T(8,128)(2,1)}, u32[]{:S(2)}) copy-start(bf16[128,4096]{0,1:T(8,128)(2,1)} %all-gather.2.cloned.1.call-done) | copy-start | bytes 3145732
  112.6 40.4 %copy-start.7 = (f32[1,4096]{1,0:T(1,128)S(1)}, f32[1,4096]{1,0:T(1,128)}, u32[]{:S(2)}) copy-start(f32[1,4096]{1,0:T(1,128)} %param.10) | copy-start | bytes 49156
  112.6 97.4 %reduce-scatter.6.cloned.1.call-start = ((), (), s32[]{:S(2)}) async-start(), calls=%async_computation.10 | async-start | bytes 786432 | tf_op jit(solution)/shard_map/reduce_scatter | solution.py:84
  113.0 58.1 %copy-start.10 = (f32[1,4]{1,0:T(1,128)S(1)}, f32[1,4]{1,0:T(1,128)}, u32[]{:S(2)}) copy-start(f32[1,4]{1,0:T(1,128)} %param.13) | copy-start | bytes 52
  151.1 1.9 copy-start.1
  186.1 1.0 copy-start.2
  187.1 22.9 %copy-start.6 = (bf16[128,1024]{1,0:T(8,128)(2,1)S(1)}, bf16[128,1024]{1,0:T(8,128)(2,1)}, u32[]{:S(2)}) copy-start(bf16[128,1024]{1,0:T(8,128)(2,1)} %reduce-scatter.4.cloned.1.call-done) | copy-start | bytes 786436
  219.0 4.6 %copy-start.4 = (bf16[256,1024]{1,0:T(8,128)(2,1)}, bf16[256,1024]{1,0:T(8,128)(2,1)S(1)}, u32[]{:S(2)}) copy-start(bf16[256,1024]{1,0:T(8,128)(2,1)S(1)} %all_gather.11) | copy-start | bytes 1572868
  223.6 16.6 %all-to-all-start.3 = ((bf16[2,128,2048]{2,1,0:T(8,128)(2,1)}), bf16[2,128,2048]{2,1,0:T(8,128)(2,1)}, u32[]{:S(2)}, u32[]{:S(2)}) async-start(bf16[2,128,2048]{2,1,0:T(8,128)(2,1)} %bitcast.105), calls=%async_computation.5 | async-start | bytes 2097152 | tf_op jit(solution)/shard_map/all_to_all | solution.py:95
  229.2 77.8 %reduce-scatter.8.cloned.1.call-start = ((), (), s32[]{:S(2)}) async-start(), calls=%async_computation.11 | async-start | bytes 1114112 | tf_op jit(solution)/shard_map/reduce_scatter | solution.py:100
  256.0 9.9 %copy-start.5 = (bf16[256,1024]{1,0:T(8,128)(2,1)S(1)}, bf16[256,1024]{1,0:T(8,128)(2,1)}, u32[]{:S(2)}) copy-start(bf16[256,1024]{1,0:T(8,128)(2,1)} %copy-done.4) | copy-start | bytes 1572868
Sparse Core Ops, SparseCore 0:
  10.7 38.4 all-gather.1
  70.1 13.9 reduce-scatter.3
  112.7 38.3 all-reduce.1
  191.7 18.2 reduce-scatter.5
  248.9 58.0 reduce-scatter.7
where the time goes:
time: 320 us; the launch traced here: 315 us
  waiting for transfers between devices  138 us (43%)
  blocking collectives  72.8 us (23%)
  matrix products  31.7 us (10%)
  other arithmetic  31.6 us (10%)
  local copies, waits for them, and re-layouts  21.4 us (7%)
  between operations  13.9 us (4%)
  starting transfers between devices  5.77 us (2%)
    all_gather x1, waiting for transfers between devices, local(): trunk_rows = lax.all_gather(hidden, ('member', 'mp'), axis=1, tiled=True)  40.4 us
    psum x1, waiting for transfers between devices, local(): lax.psum(branch.astype(jnp.bfloat16), 'mp').astype(jnp.float32)  38.1 us
    reduce_sum x2, other arithmetic, slab_terms(): return jnp.sum(rounded.astype(jnp.float32), axis=0)  19.4 us
    reduce_scatter x1, waiting for transfers between devices, local(): lax.psum_scatter(lax.dot_general(rows_here, w_second, AGAINST, preferred_...  18.4 us
    reduce_scatter x1, waiting for transfers between devices, local(): lax.psum_scatter(hidden_term.astype(jnp.bfloat16), ('member', 'mp'), scat...  16.6 us
    all_to_all x1, blocking collectives, local(): lax.all_to_all(trunk_rows, 'dp', split_axis=1, concat_axis=0, tiled=True)  15 us
    all_to_all x1, blocking collectives, local(): lax.all_to_all(branch_cols.astype(jnp.bfloat16), 'dp', split_axis=0, conc...  14.5 us
    reduce_scatter x1, waiting for transfers between devices, local(): lax.psum_scatter(jnp.dot(rows_here, w_first, preferred_element_type=jnp.f...  14 us
  transfers between devices with their start and end apart: 6, of which 6 were waited for; matrix products, arithmetic and copies ran while one was open for 13% of the time, Pallas kernels for 0%

commit v1 on v0

v1 whole, which is shorter than its diff:
```python
import functools

import jax
import jax.numpy as jnp
from jax import lax
from jax.experimental import pallas as pl
from jax.experimental.pallas import tpu as pltpu
from jax.sharding import PartitionSpec as P

PENALTY = 0.5
SPREAD_FLOOR = 0.25
EPSILON = 1e-05
MESH = pl.DeviceIdType.MESH
AGAINST = (((1,), (1,)), ((), ()))
ALONG = (((0,), (0,)), ((), ()))
F32 = jnp.float32
BF16 = jnp.bfloat16
LANES = 128
CORES = 2
TILE = 256


def dot(a, b):
    return jnp.dot(a, b, preferred_element_type=F32)


def dot_nt(a, b):
    return lax.dot_general(a, b, AGAINST, preferred_element_type=F32)


def sigmoid(v):
    return 1.0 / (1.0 + jnp.exp(-v))


def trunk_kernel(
    sizes,
    len_ref, off_ref, sw_ref, hid_ref, vec_ref, win_hbm, wout_hbm,
    pen_out, gh_out, h_out, act_out, sh_out, bg_out,
    win, wout, z, h, pool, gp, gs, gr, act, bp, bs, br, xr, cs, cr, ps, sc, pens,
    sf, sh, bk, ks, bg, fs, fr, fo, x2s, x2r, ts, zr,
    local_sem, out_sem, send_sem, z_sem, h_sem, pool_sem, g_sem, b_sem, x_sem, c_sem,
    sc_send, sc_recv, k_sem, f_sem, x2_sem, t_send, t_recv,
):
    dp, members, mp, tokens, chunk, ff, seqs, features = sizes
    nh = mp // CORES
    mloc = members // dp
    half = mloc * mp * chunk // CORES
    d = lax.axis_index("dp")
    m = lax.axis_index("member")
    p = lax.axis_index("mp")
    hi = p // CORES
    lo = p % CORES
    sib = hi * CORES + (1 - lo)

    def device(dd, mm, pp):
        return {"dp": dd, "member": mm, "mp": pp}

    def hsem(q, j, s):
        return h_sem.at[(q * mloc + j) * dp + s]

    sent = []

    def push(src, dst, sem, to):
        copy = pltpu.make_async_remote_copy(
            src_ref=src, dst_ref=dst, send_sem=send_sem.at[len(sent)], recv_sem=sem,
            device_id=to, device_id_type=MESH,
        )
        copy.start()
        sent.append(copy)

    def arrived(ref, sem):
        pltpu.make_async_copy(ref, ref, sem).wait()

    load_in = pltpu.make_async_copy(win_hbm.at[0], win, local_sem.at[0])
    load_out = pltpu.make_async_copy(wout_hbm.at[0], wout, local_sem.at[1])
    load_in.start()
    load_out.start()

    group = [
        (a, b, c)
        for a in range(dp) for b in range(members) for c in range(CORES)
        if (a, b, c) != (0, 0, 0)
    ]

    def relative(a, b, c):
        return (
            lax.rem(d + a, dp), lax.rem(m + b, members), lax.rem(lo + c, CORES)
        )

    others_hi = [lax.rem(hi + r, nh) for r in range(1, nh)]
    others_d = [lax.rem(d + r, dp) for r in range(1, dp)]
    barrier = pltpu.get_barrier_semaphore()
    for a, b, c in group:
        dd, mm, cc = relative(a, b, c)
        pl.semaphore_signal(
            barrier, inc=1, device_id=device(dd, mm, hi * CORES + cc), device_id_type=MESH
        )
    for hh in others_hi:
        pl.semaphore_signal(
            barrier, inc=1, device_id=device(d, m, hh * CORES + lo), device_id_type=MESH
        )
    pl.semaphore_wait(barrier, len(group) + nh - 1)

    pltpu.make_async_copy(hid_ref, z.at[m], z_sem.at[m]).start()
    for r in range(1, members):
        push(hid_ref, z.at[m], z_sem.at[m], device(d, lax.rem(m + r, members), p))

    place = lax.broadcasted_iota(jnp.int32, (1, tokens), 1)
    row = lax.broadcasted_iota(jnp.int32, (8, tokens), 0)
    pooled = jnp.zeros((8, tokens), F32)
    weights = jnp.zeros((8, tokens), F32)
    start = jnp.int32(0)
    for i in range(seqs):
        size = len_ref[0, i]
        target = start + lax.rem(off_ref[0, i], size)
        inside = jnp.where((place >= start) & (place < start + size), 1.0, 0.0)
        value = inside / jnp.full((1, tokens), size, jnp.int32).astype(F32)
        value = value + jnp.where(place == target, 1.0, 0.0)
        pooled = jnp.where(row == i, value, pooled)
        weights = jnp.where(row == i, sw_ref[0, i], weights)
        start = start + size
    pool[d, 0] = pooled
    pool[d, 1] = weights
    for dd in others_d:
        push(pool.at[d], pool.at[d], pool_sem.at[d], device(dd, m, p))

    for dd in others_d:
        for j in range(mloc):
            c = dd * mloc + j
            arrived(z.at[c], z_sem.at[c])
            push(z.at[c], h.at[p, j, d], hsem(p, j, d), device(dd, m, p))
    for j in range(mloc):
        c = d * mloc + j
        arrived(z.at[c], z_sem.at[c])
        for hh in others_hi:
            push(z.at[c], h.at[p, j, d], hsem(p, j, d), device(d, m, hh * CORES + lo))
        push(z.at[c], h.at[p, j, d], hsem(p, j, d), device(d, m, sib))
        pltpu.make_async_copy(z.at[c], h.at[p, j, d], hsem(p, j, d)).start()
    for dd in others_d:
        for j in range(mloc):
            arrived(h.at[p, j, dd], hsem(p, j, dd))
            for hh in others_hi:
                push(h.at[p, j, dd], h.at[p, j, dd], hsem(p, j, dd), device(d, m, hh * CORES + lo))
            push(h.at[p, j, dd], h.at[p, j, dd], hsem(p, j, dd), device(d, m, sib))
    for j in range(mloc):
        arrived(h.at[p, j, d], hsem(p, j, d))

    def gate_rows(q, j):
        return pl.ds(pl.multiple_of((j * mp + q) * chunk, chunk), chunk)

    def gate_add(q, first):
        for c in range(0, ff, TILE):
            total = None
            for j in range(mloc):
                left = h[q, j].reshape(dp * tokens, chunk)
                term = dot(left, win[gate_rows(q, j), c:c + TILE])
                total = term if total is None else total + term
            total = total.reshape(dp, tokens, TILE)
            if not first:
                total = total + gp[:, :, c:c + TILE]
            gp[:, :, c:c + TILE] = total

    def all_here(q):
        for j in range(mloc):
            for s in range(dp):
                arrived(h.at[q, j, s], hsem(q, j, s))

    load_in.wait()
    gate_add(p, True)
    all_here(sib)
    gate_add(sib, False)
    for hh in others_hi:
        q = hh * CORES + lo
        for j in range(mloc):
            for s in range(dp):
                arrived(h.at[q, j, s], hsem(q, j, s))
                push(h.at[q, j, s], h.at[q, j, s], hsem(q, j, s), device(d, m, sib))
        gate_add(q, False)
    for k, hh in enumerate(others_hi):
        q = hh * CORES + (1 - lo)
        all_here(q)
        if k < len(others_hi) - 1:
            gate_add(q, False)
            continue
        for s in range(dp):
            for c in range(0, ff, TILE):
                total = gp[s, :, c:c + TILE]
                for j in range(mloc):
                    total = total + dot(h[q, j, s], win[gate_rows(q, j), c:c + TILE])
                gp[s, :, c:c + TILE] = total
                gs[s, :, c:c + TILE] = total.astype(BF16)
            for slot, dd in enumerate(others_d):
                slot = dp - 2 - slot
                push(gs.at[s], gr.at[s, slot], g_sem.at[s * dp + slot], device(dd, m, p))
    keep_h = pltpu.make_async_copy(h, h_out, out_sem.at[0])
    keep_h.start()

    load_out.wait()
    for s in range(dp):
        for slot in range(dp - 1):
            arrived(gr.at[s, slot], g_sem.at[s * dp + slot])
        for c in range(0, ff, TILE):
            gate = gp[s, :, c:c + TILE]
            for slot in range(dp - 1):
                gate = gate + gr[s, slot, :, c:c + TILE].astype(F32)
            gp[s, :, c:c + TILE] = gate
            act[s, :, c:c + TILE] = (gate * sigmoid(gate)).astype(BF16)
        for c in range(0, half, TILE):
            cols = pl.ds(pl.multiple_of((1 - lo) * half + c, TILE), TILE)
            bs[s, :, c:c + TILE] = dot(act[s], wout[:, cols]).astype(BF16)
        push(bs.at[s], br.at[s], b_sem.at[s], device(d, m, sib))
        for c in range(0, half, TILE):
            cols = pl.ds(pl.multiple_of(lo * half + c, TILE), TILE)
            bp[s, :, c:c + TILE] = dot(act[s], wout[:, cols])
        arrived(br.at[s], b_sem.at[s])
        xr[s, hi] = (bp[s] + br[s].astype(F32)).astype(BF16)
        for hh in others_hi:
            push(xr.at[s, hi], xr.at[s, hi], x_sem.at[s * nh + hi], device(d, m, hh * CORES + lo))
    keep_act = pltpu.make_async_copy(act, act_out, out_sem.at[1])
    keep_act.start()

    lane = lax.broadcasted_iota(jnp.int32, (tokens, LANES), 1)
    for s in range(dp):
        for hh in others_hi:
            arrived(xr.at[s, hh], x_sem.at[s * nh + hh])
        squares = jnp.zeros((tokens, 1), F32)
        along = jnp.zeros((tokens, 1), F32)
        for k in range(half // chunk):
            block = lo * (half // chunk) + k
            c = k * chunk
            branch = xr[s, 0, :, c:c + chunk].astype(F32)
            for hh in range(1, nh):
                branch = branch + xr[s, hh, :, c:c + chunk].astype(F32)
            comb = h[block % mp, block // mp, s].astype(F32) + branch
            bp[s, :, c:c + chunk] = comb
            cs[s, :, c:c + chunk] = comb.astype(BF16)
            cols = pl.ds(pl.multiple_of((d * CORES + lo) * half + c, chunk), chunk)
            squares = squares + jnp.sum(comb * comb, axis=1, keepdims=True)
            along = along + jnp.sum(comb * vec_ref[:, cols], axis=1, keepdims=True)
        both = jnp.where(lane == 0, squares, along)
        ps[s] = jnp.transpose(both)[:8]
        mine = (m * dp + d) * CORES + lo
        pltpu.make_async_copy(ps.at[s], sc.at[s, mine], sc_recv.at[s]).start()
        for a, b, c in group:
            dd, mm, cc = relative(a, b, c)
            pltpu.make_async_remote_copy(
                src_ref=ps.at[s], dst_ref=sc.at[s, mine],
                send_sem=sc_send.at[s], recv_sem=sc_recv.at[s],
                device_id=device(dd, mm, hi * CORES + cc), device_id_type=MESH,
            ).start()
        push(cs.at[s], cr.at[s], c_sem.at[s], device(d, m, sib))

    for dd in others_d:
        arrived(pool.at[dd], pool_sem.at[dd])
    for s in range(dp):
        arrived(sc.at[s], sc_recv.at[s])
        pooled = pool[s, 0]

        def head(mm):
            total = sc[s, mm * dp * CORES]
            for i in range(1, dp * CORES):
                total = total + sc[s, mm * dp * CORES + i]
            inv = lax.rsqrt(total[0:1] / features + EPSILON)
            score = total[1:2] * inv
            return inv, score, jnp.sum(score * pooled, axis=1, keepdims=True)

        rewards = [head(mm)[2] for mm in range(members)]
        center = rewards[0]
        for mm in range(1, members):
            center = center + rewards[mm]
        center = center / members
        spread = (rewards[0] - center) ** 2
        for mm in range(1, members):
            spread = spread + (rewards[mm] - center) ** 2
        deviation = jnp.sqrt(spread / members + SPREAD_FLOOR)
        pens[s] = jnp.broadcast_to(center - PENALTY * deviation, (8, LANES))
        inv, score, reward = head(m)
        pull = pool[s, 1] * (1.0 - PENALTY * (reward - center) / deviation) / members
        weight = jnp.sum(pooled * pull, axis=0, keepdims=True)
        by_vec = weight * inv
        by_comb = weight * (score * inv * inv / features)
        rows = lax.broadcasted_iota(jnp.int32, (LANES, tokens), 0)
        both = jnp.transpose(jnp.where(rows == 0, by_vec, by_comb))
        by_vec, by_comb = both[:, 0:1], both[:, 1:2]
        arrived(cr.at[s], c_sem.at[s])
        for own in (True, False):
            base = lo * half if own else (1 - lo) * half
            for c in range(0, half, TILE):
                comb = bp[s, :, c:c + TILE] if own else cr[s, :, c:c + TILE].astype(F32)
                vec = vec_ref[:, pl.ds(pl.multiple_of(d * CORES * half + base + c, TILE), TILE)]
                slope = by_vec * vec - by_comb * comb
                cols = pl.ds(pl.multiple_of(base + c, TILE), TILE)
                sf[s, :, cols] = slope
                sh[s, :, cols] = slope.astype(BF16)
        for c in range(0, ff, TILE):
            term = dot_nt(sh[s], wout[c:c + TILE, :])
            bk[s, :, c:c + TILE] = term
            ks[s, :, c:c + TILE] = term.astype(BF16)
        for slot, dd in enumerate(others_d):
            slot = dp - 2 - slot
            push(ks.at[s], gr.at[s, slot], k_sem.at[s * dp + slot], device(dd, m, p))
    keep_sh = pltpu.make_async_copy(sh, sh_out, out_sem.at[2])
    keep_sh.start()
    spot = lax.broadcasted_iota(jnp.int32, (8, LANES), 1)
    diag = lax.broadcasted_iota(jnp.int32, (8, LANES), 0) == spot
    flat = jnp.sum(jnp.where(diag, pens[d], 0.0), axis=0, keepdims=True)
    pen_out[...] = flat[:, :seqs]

    for s in range(dp):
        for slot in range(dp - 1):
            arrived(gr.at[s, slot], k_sem.at[s * dp + slot])
        for c in range(0, ff, TILE):
            raw = bk[s, :, c:c + TILE]
            for slot in range(dp - 1):
                raw = raw + gr[s, slot, :, c:c + TILE].astype(F32)
            gate = gp[s, :, c:c + TILE]
            sig = sigmoid(gate)
            bg[s, :, c:c + TILE] = (raw * (sig * (1.0 + gate * (1.0 - sig)))).astype(BF16)

        def hidden_term(hh, j, cc):
            first = (j * mp + hh * CORES + cc) * chunk
            return dot_nt(bg[s], win[pl.ds(pl.multiple_of(first, chunk), chunk), :])

        for hh in range(nh):
            for j in range(mloc):
                fs[s, hh, j] = hidden_term(hh, j, 1 - lo).astype(BF16)
        push(fs.at[s], fr.at[s], f_sem.at[s], device(d, m, sib))
        for hh in range(nh):
            for j in range(mloc):
                fo[s, hh, j] = hidden_term(hh, j, lo)
        arrived(fr.at[s], f_sem.at[s])
        for hh in others_hi:
            x2s[s, hh] = (fo[s, hh] + fr[s, hh].astype(F32)).astype(BF16)
            push(x2s.at[s, hh], x2r.at[s, hi], x2_sem.at[s * nh + hi], device(d, m, hh * CORES + lo))
    keep_bg = pltpu.make_async_copy(bg, bg_out, out_sem.at[3])
    keep_bg.start()

    last = []
    for s in range(dp):
        for hh in others_hi:
            arrived(x2r.at[s, hh], x2_sem.at[s * nh + hh])
        for j in range(mloc):
            total = fo[s, hi, j] + fr[s, hi, j].astype(F32)
            for hh in others_hi:
                total = total + x2r[s, hh, j].astype(F32)
            cols = pl.ds(pl.multiple_of((j * mp + p) * chunk, chunk), chunk)
            ts[s, j] = (total + sf[s, :, cols]).astype(BF16)
            to = d * mloc + j
            here = jnp.logical_and(d == s, to == m)
            away = pltpu.make_async_remote_copy(
                src_ref=ts.at[s, j], dst_ref=zr.at[m],
                send_sem=t_send.at[s * mloc + j], recv_sem=t_recv.at[m],
                device_id=device(jnp.int32(s), to, p), device_id_type=MESH,
            )
            near = pltpu.make_async_copy(ts.at[s, j], zr.at[m], t_recv.at[m])

            @pl.when(here)
            def _(near=near):
                near.start()

            @pl.when(jnp.logical_not(here))
            def _(away=away):
                away.start()

            last.append((here, away))

    arrived(zr.at[0], t_recv.at[0])
    total = zr[0].astype(F32)
    for mm in range(1, members):
        arrived(zr.at[mm], t_recv.at[mm])
        total = total + zr[mm].astype(F32)
    gh_out[...] = total

    for copy in sent:
        copy.wait_send()
    for here, away in last:
        @pl.when(jnp.logical_not(here))
        def _(away=away):
            away.wait_send()
    for s in range(dp):
        some = sc.at[s, pl.ds(0, len(group))]
        pltpu.make_async_copy(some, some, sc_send.at[s]).wait()
    for copy in (keep_h, keep_act, keep_sh, keep_bg):
        copy.wait()


def weight_kernel(slabs, h_ref, bg_ref, act_ref, sh_ref, gin_ref, gout_ref):
    def terms(left, right):
        total = None
        for s in range(slabs):
            term = lax.dot_general(left(s), right[s], ALONG, preferred_element_type=F32)
            term = term.astype(BF16).astype(F32)
            total = term if total is None else total + term
        return total

    gin_ref[0] = terms(lambda s: h_ref[0, 0, s], bg_ref)
    gout_ref[0] = terms(lambda s: act_ref[s], sh_ref)


def solution(mesh):
    dp, members, mp = mesh.shape["dp"], mesh.shape["member"], mesh.shape["mp"]

    def local(hidden, w_in, w_out, score_vec, lengths, reward_offset, seq_weight):
        tokens, chunk = hidden.shape
        _, rows, ff = w_in.shape
        seqs = lengths.shape[1]
        features = score_vec.shape[1]
        nh = mp // CORES
        mloc = members // dp
        half = rows // CORES
        peers = dp * members * CORES
        sizes = (dp, members, mp, tokens, chunk, ff, seqs, features)
        smem = pl.BlockSpec(memory_space=pltpu.SMEM)
        vmem = pl.BlockSpec(memory_space=pltpu.VMEM)
        hbm = pl.BlockSpec(memory_space=pl.ANY)
        V = pltpu.VMEM
        dma = lambda n: pltpu.SemaphoreType.DMA((n,))
        sds = jax.ShapeDtypeStruct
        flops = 8 * dp * tokens * rows * ff
        pen, gh, h, act, sh, bg = pl.pallas_call(
            functools.partial(trunk_kernel, sizes),
            out_shape=(
                sds((1, seqs), F32),
                sds((tokens, chunk), F32),
                sds((mp, mloc, dp, tokens, chunk), BF16),
                sds((dp, tokens, ff), BF16),
                sds((dp, tokens, rows), BF16),
                sds((dp, tokens, ff), BF16),
            ),
            in_specs=[smem, smem, smem, hbm, vmem, hbm, hbm],
            out_specs=(vmem, vmem, hbm, hbm, hbm, hbm),
            scratch_shapes=[
                V((rows, ff), BF16),
                V((ff, rows), BF16),
                V((members, tokens, chunk), BF16),
                V((mp, mloc, dp, tokens, chunk), BF16),
                V((dp, 2, 8, tokens), F32),
                V((dp, tokens, ff), F32),
                V((dp, tokens, ff), BF16),
                V((dp, dp - 1, tokens, ff), BF16),
                V((dp, tokens, ff), BF16),
                V((dp, tokens, half), F32),
                V((dp, tokens, half), BF16),
                V((dp, tokens, half), BF16),
                V((dp, nh, tokens, half), BF16),
                V((dp, tokens, half), BF16),
                V((dp, tokens, half), BF16),
                V((dp, 8, tokens), F32),
                V((dp, peers, 8, tokens), F32),
                V((dp, 8, LANES), F32),
                V((dp, tokens, rows), F32),
                V((dp, tokens, rows), BF16),
                V((dp, tokens, ff), F32),
                V((dp, tokens, ff), BF16),
                V((dp, tokens, ff), BF16),
                V((dp, nh, mloc, tokens, chunk), BF16),
                V((dp, nh, mloc, tokens, chunk), BF16),
                V((dp, nh, mloc, tokens, chunk), F32),
                V((dp, nh, mloc, tokens, chunk), BF16),
                V((dp, nh, mloc, tokens, chunk), BF16),
                V((dp, mloc, tokens, chunk), BF16),
                V((members, tokens, chunk), BF16),
                dma(2), dma(4), dma(128), dma(members), dma(mp * mloc * dp), dma(dp),
                dma(dp * dp), dma(dp), dma(dp * nh), dma(dp), dma(dp), dma(dp),
                dma(dp * dp), dma(dp), dma(dp * nh), dma(dp * mloc), dma(members),
            ],
            compiler_params=pltpu.CompilerParams(
                collective_id=0, has_side_effects=True, vmem_limit_bytes=60 * 2**20
            ),
            cost_estimate=pl.CostEstimate(
                flops=flops, bytes_accessed=4 * rows * ff, transcendentals=0
            ),
        )(lengths, reward_offset, seq_weight, hidden, score_vec, w_in, w_out)

        steps = mloc * mp
        out_rows = ff // steps
        whole = lambda *shape: pl.BlockSpec(shape, lambda i: (0,) * len(shape))
        gin, gout = pl.pallas_call(
            functools.partial(weight_kernel, dp),
            grid=(steps,),
            out_shape=(sds((1, rows, ff), F32), sds((1, ff, rows), F32)),
            in_specs=[
                pl.BlockSpec((1, 1, dp, tokens, chunk), lambda i: (i % mp, i // mp, 0, 0, 0)),
                whole(dp, tokens, ff),
                pl.BlockSpec((dp, tokens, out_rows), lambda i: (0, 0, i)),
                whole(dp, tokens, rows),
            ],
            out_specs=(
                pl.BlockSpec((1, chunk, ff), lambda i: (0, i, 0)),
                pl.BlockSpec((1, out_rows, rows), lambda i: (0, i, 0)),
            ),
            compiler_params=pltpu.CompilerParams(vmem_limit_bytes=40 * 2**20),
            cost_estimate=pl.CostEstimate(
                flops=flops // 2, bytes_accessed=8 * rows * ff, transcendentals=0
            ),
        )(h, bg, act, sh)
        return pen, gh, gin, gout

    in_specs = (
        P("dp", ("member", "mp")),
        P("member", "dp", "mp"),
        P("member", "mp", "dp"),
        P("member", None),
        P("dp", None),
        P("dp", None),
        P("dp", None),
    )
    out_specs = (
        P("dp", None),
        P("dp", ("member", "mp")),
        P("member", "dp", "mp"),
        P("member", "mp", "dp"),
    )
    return jax.shard_map(local, mesh=mesh, in_specs=in_specs, out_specs=out_specs, check_vma=False)
```

time: 320 us -> 92 us (0.29); the launches traced: 315 us -> 90.8 us
  waiting for transfers between devices: 138 us -> 0 us
  Pallas kernels: 0 us -> 83 us
  blocking collectives: 72.8 us -> 0 us
  matrix products: 31.7 us -> 0 us
  other arithmetic: 31.6 us -> 0 us
  local copies, waits for them, and re-layouts: 21.4 us -> 7.22 us
  between operations: 13.9 us -> 0.65 us
  starting transfers between devices: 5.77 us -> 0 us
    pallas_call x0 -> x2, Pallas kernels: none -> 83 us  [the longest x1 75 us: local(): pl.pallas_call(functools.partial(trunk_kernel, sizes), out_shape=(sds((1,...]
    reduce_scatter x3 -> x0, waiting for transfers between devices: 49 us -> none  [the longest x1 18.4 us: local(): lax.psum_scatter(lax.dot_general(rows_here, w_second, AGAINST, preferred_...]
    all_to_all x3 -> x0, blocking collectives: 40.6 us -> none  [the longest x1 15 us: local(): lax.all_to_all(trunk_rows, 'dp', split_axis=1, concat_axis=0, tiled=True)]
    all_gather x1 -> x0, waiting for transfers between devices: 40.4 us -> none  [local(): trunk_rows = lax.all_gather(hidden, ('member', 'mp'), axis=1, tiled=True)]
    psum x1 -> x0, waiting for transfers between devices: 38.1 us -> none  [local(): lax.psum(branch.astype(jnp.bfloat16), 'mp').astype(jnp.float32)]
    dot_general x9 -> x0, matrix products: 31.7 us -> none  [the longest x2 12.9 us: slab_terms(): jnp.einsum('bsd,bsf->bdf', left_blocks, right_blocks, preferred_element_t...]
    reduce_sum x3 -> x0, other arithmetic: 21.3 us -> none  [the longest x2 19.4 us: slab_terms(): return jnp.sum(rounded.astype(jnp.float32), axis=0)]
    psum x2 -> x0, blocking collectives: 16.5 us -> none  [the longest x1 9.61 us: local(): spread = lax.psum((rewards - center) ** 2, 'member') / members]
  transfers between devices with their start and end apart: 6 -> 0, of which waited for: 6 -> 0; matrix products, arithmetic and copies ran while one was open for 13% -> 0% of each run, Pallas kernels for 0% -> 0%
where the time goes in v1:
time: 92 us; the launch traced here: 90.8 us
  Pallas kernels  83 us (90%)
  local copies, waits for them, and re-layouts  7.22 us (8%)
    pallas_call x1, Pallas kernels, local(): pl.pallas_call(functools.partial(trunk_kernel, sizes), out_shape=(sds((1,...  75 us
    pallas_call x1, Pallas kernels, local(): pl.pallas_call(functools.partial(weight_kernel, dp), grid=(steps,), out_s...  7.95 us
    unnamed x10, local copies, waits for them, and re-layouts  7.22 us

profile of v1, /device:TPU:13, one launch (start us, length us, event | category | flops | bytes accessed | tf_op | source)
XLA Modules:
  0.0 90.8 jit_solution(14923210617631813068)
XLA Ops:
  0.6 75.0 %shard_map.102 = (f32[1,4]{1,0:T(1,128)}, f32[128,256]{1,0:T(8,128)}, bf16[4,2,2,128,256]{4,3,2,1,0:T(8,128)(2,1)}, bf16[2,128,1024]{2,1,0:T(8,128)(2,1)}, bf16[...) custom-call(s32[1,4]{1,0:T(1,128)} %len_ref.1, s32[1,4]{1,0:T(1,128)} %off_ref.1, f32[1,4]{1,0:T(1,128)} %sw_ref.1, ...), custom_call_target="tpu_custom_call" | custom-call | flops 4294967296 | bytes 8388608 | tf_op jit(solution)/shard_map/pallas_call | solution.py:420
  75.6 0.0 copy-start
  75.7 1.2 %copy-done = bf16[4,2,2,128,256]{4,3,2,1,0:T(8,128)(2,1)S(1)} copy-done((bf16[4,2,2,128,256]{4,3,2,1,0:T(8,128)(2,1)S(1)}, bf16[4,2,2,128,256]{4,3,2,1,0:T(8,128)(2,1)}, u32[]{:S(2)}) %copy-start) | copy-done | bytes 1048600
  76.9 0.0 copy-start.1
  76.9 1.2 %copy-done.1 = bf16[2,128,2048]{2,1,0:T(8,128)(2,1)S(1)} copy-done((bf16[2,128,2048]{2,1,0:T(8,128)(2,1)S(1)}, bf16[2,128,2048]{2,1,0:T(8,128)(2,1)}, u32[]{:S(2)}) %copy-start.1) | copy-done | bytes 1048600
  78.1 0.0 copy-start.2
  78.1 1.0 %copy-done.2 = bf16[2,128,1024]{2,1,0:T(8,128)(2,1)S(1)} copy-done((bf16[2,128,1024]{2,1,0:T(8,128)(2,1)S(1)}, bf16[2,128,1024]{2,1,0:T(8,128)(2,1)}, u32[]{:S(2)}) %copy-start.2) | copy-done | bytes 524312
  79.1 0.0 copy-start.3
  79.1 1.0 %copy-done.3 = bf16[2,128,1024]{2,1,0:T(8,128)(2,1)S(1)} copy-done((bf16[2,128,1024]{2,1,0:T(8,128)(2,1)S(1)}, bf16[2,128,1024]{2,1,0:T(8,128)(2,1)}, u32[]{:S(2)}) %copy-start.3) | copy-done | bytes 524312
  80.2 8.0 %shard_map.103 = (f32[1,2048,1024]{2,1,0:T(8,128)}, f32[1,1024,2048]{2,1,0:T(8,128)}) custom-call(bf16[4,2,2,128,256]{4,3,2,1,0:T(8,128)(2,1)S(1)} %copy-done, bf16[2,128,1024]{2,1,0:T(8,128)(2,1)S(1)} %copy-done.3, bf16[2,128,1024]{2,1,0:T(8,128)(2,1)S(1)} %copy-done.2, bf16[2,128,2048]{2,1,0:T(8,128)(2,1)S(1)} %copy-done.1), custom_call_target="tpu_custom_call" | custom-call | flops 2147483648 | bytes 16777216 | tf_op jit(solution)/shard_map/pallas_call | solution.py:478
  88.1 1.1 %copy.13 = f32[1,4]{1,0:T(1,128)} copy(f32[1,4]{1,0:T(1,128)} %get-tuple-element.24) | data formatting | bytes 32
  89.3 1.6 %copy.14 = f32[128,256]{1,0:T(8,128)} copy(f32[128,256]{1,0:T(8,128)} %get-tuple-element.25) | data formatting | bytes 262144
Async XLA Ops:
  75.6 1.2 %copy-start = (bf16[4,2,2,128,256]{4,3,2,1,0:T(8,128)(2,1)S(1)}, bf16[4,2,2,128,256]{4,3,2,1,0:T(8,128)(2,1)}, u32[]{:S(2)}) copy-start(bf16[4,2,2,128,256]{4,3,2,1,0:T(8,128)(2,1)} %get-tuple-element.14.h_ref) | copy-start | bytes 3145732
  76.9 1.2 %copy-start.1 = (bf16[2,128,2048]{2,1,0:T(8,128)(2,1)S(1)}, bf16[2,128,2048]{2,1,0:T(8,128)(2,1)}, u32[]{:S(2)}) copy-start(bf16[2,128,2048]{2,1,0:T(8,128)(2,1)} %get-tuple-element.17.sh_ref) | copy-start | bytes 3145732
  78.1 1.0 %copy-start.2 = (bf16[2,128,1024]{2,1,0:T(8,128)(2,1)S(1)}, bf16[2,128,1024]{2,1,0:T(8,128)(2,1)}, u32[]{:S(2)}) copy-start(bf16[2,128,1024]{2,1,0:T(8,128)(2,1)} %get-tuple-element.16.act_ref) | copy-start | bytes 1572868
  79.1 1.0 %copy-start.3 = (bf16[2,128,1024]{2,1,0:T(8,128)(2,1)S(1)}, bf16[2,128,1024]{2,1,0:T(8,128)(2,1)}, u32[]{:S(2)}) copy-start(bf16[2,128,1024]{2,1,0:T(8,128)(2,1)} %get-tuple-element.15.bg_ref) | copy-start | bytes 1572868

commit v2 on v1

--- a/solution.py
+++ b/solution.py
@@ -35,11 +35,25 @@
 def trunk_kernel(
     sizes,
     len_ref, off_ref, sw_ref, hid_ref, vec_ref, win_hbm, wout_hbm,
-    pen_out, gh_out, h_out, act_out, sh_out, bg_out,
+    *rest,
+):
+    members = sizes[1]
+    pen_out, h_out, act_out, sh_out, bg_out = rest[:5]
+    chunk_outs = rest[5:5 + members]
+    trunk_body(
+        sizes, len_ref, off_ref, sw_ref, hid_ref, vec_ref, win_hbm, wout_hbm,
+        pen_out, h_out, act_out, sh_out, bg_out, chunk_outs, *rest[5 + members:]
+    )
+
+
+def trunk_body(
+    sizes,
+    len_ref, off_ref, sw_ref, hid_ref, vec_ref, win_hbm, wout_hbm,
+    pen_out, h_out, act_out, sh_out, bg_out, chunk_outs,
     win, wout, z, h, pool, gp, gs, gr, act, bp, bs, br, xr, cs, cr, ps, sc, pens,
-    sf, sh, bk, ks, bg, fs, fr, fo, x2s, x2r, ts, zr,
+    sf, sh, bk, ks, bg, fs, fr, fo, x2s, x2r,
     local_sem, out_sem, send_sem, z_sem, h_sem, pool_sem, g_sem, b_sem, x_sem, c_sem,
-    sc_send, sc_recv, k_sem, f_sem, x2_sem, t_send, t_recv,
+    sc_send, sc_recv, k_sem, f_sem, x2_sem,
 ):
     dp, members, mp, tokens, chunk, ff, seqs, features = sizes
     nh = mp // CORES
@@ -67,6 +81,7 @@
         )
         copy.start()
         sent.append(copy)
+        return copy
 
     def arrived(ref, sem):
         pltpu.make_async_copy(ref, ref, sem).wait()
@@ -165,6 +180,21 @@
             for s in range(dp):
                 arrived(h.at[q, j, s], hsem(q, j, s))
 
+    waited = []
+    tiles = ff // TILE
+
+    def tile_sem(sem, s, slot, t):
+        return sem.at[(s * dp + slot) * tiles + t]
+
+    def send_tile(src, s, t, sem):
+        copies = []
+        for k, dd in enumerate(others_d):
+            slot = dp - 2 - k
+            copies.append(push(
+                src.at[s, t], gr.at[s, slot, t], tile_sem(sem, s, slot, t), device(dd, m, p)
+            ))
+        return copies
+
     load_in.wait()
     gate_add(p, True)
     all_here(sib)
@@ -182,55 +212,66 @@
         if k < len(others_hi) - 1:
             gate_add(q, False)
             continue
+        early = {}
         for s in range(dp):
-            for c in range(0, ff, TILE):
-                total = gp[s, :, c:c + TILE]
+            for t in range(ff // TILE):
+                cols = slice(t * TILE, (t + 1) * TILE)
+                total = gp[s, :, cols]
                 for j in range(mloc):
-                    total = total + dot(h[q, j, s], win[gate_rows(q, j), c:c + TILE])
-                gp[s, :, c:c + TILE] = total
-                gs[s, :, c:c + TILE] = total.astype(BF16)
-            for slot, dd in enumerate(others_d):
-                slot = dp - 2 - slot
-                push(gs.at[s], gr.at[s, slot], g_sem.at[s * dp + slot], device(dd, m, p))
+                    total = total + dot(h[q, j, s], win[gate_rows(q, j), cols])
+                gp[s, :, cols] = total
+                gs[s, t] = total.astype(BF16)
+                for copy in early.pop((s - 1, t), ()):
+                    copy.wait_send()
+                    waited.append(copy)
+                early[s, t] = send_tile(gs, s, t, g_sem)
     keep_h = pltpu.make_async_copy(h, h_out, out_sem.at[0])
     keep_h.start()
 
     load_out.wait()
+    halves = half // TILE
     for s in range(dp):
-        for slot in range(dp - 1):
-            arrived(gr.at[s, slot], g_sem.at[s * dp + slot])
-        for c in range(0, ff, TILE):
-            gate = gp[s, :, c:c + TILE]
+        for t in range(tiles):
+            cols = slice(t * TILE, (t + 1) * TILE)
+            gate = gp[s, :, cols]
             for slot in range(dp - 1):
-                gate = gate + gr[s, slot, :, c:c + TILE].astype(F32)
-            gp[s, :, c:c + TILE] = gate
-            act[s, :, c:c + TILE] = (gate * sigmoid(gate)).astype(BF16)
-        for c in range(0, half, TILE):
-            cols = pl.ds(pl.multiple_of((1 - lo) * half + c, TILE), TILE)
-            bs[s, :, c:c + TILE] = dot(act[s], wout[:, cols]).astype(BF16)
-        push(bs.at[s], br.at[s], b_sem.at[s], device(d, m, sib))
-        for c in range(0, half, TILE):
-            cols = pl.ds(pl.multiple_of(lo * half + c, TILE), TILE)
-            bp[s, :, c:c + TILE] = dot(act[s], wout[:, cols])
-        arrived(br.at[s], b_sem.at[s])
-        xr[s, hi] = (bp[s] + br[s].astype(F32)).astype(BF16)
-        for hh in others_hi:
-            push(xr.at[s, hi], xr.at[s, hi], x_sem.at[s * nh + hi], device(d, m, hh * CORES + lo))
+                arrived(gr.at[s, slot, t], tile_sem(g_sem, s, slot, t))
+                gate = gate + gr[s, slot, t].astype(F32)
+            gp[s, :, cols] = gate
+            act[s, :, cols] = (gate * sigmoid(gate)).astype(BF16)
+        for t in range(halves):
+            cols = pl.ds(pl.multiple_of((1 - lo) * half + t * TILE, TILE), TILE)
+            bs[s, t] = dot(act[s], wout[:, cols]).astype(BF16)
+            push(bs.at[s, t], br.at[s, t], b_sem.at[s * halves + t], device(d, m, sib))
+        for t in range(halves):
+            cols = pl.ds(pl.multiple_of(lo * half + t * TILE, TILE), TILE)
+            term = dot(act[s], wout[:, cols])
+            arrived(br.at[s, t], b_sem.at[s * halves + t])
+            xr[s, hi, t] = (term + br[s, t].astype(F32)).astype(BF16)
+            for hh in others_hi:
+                push(
+                    xr.at[s, hi, t], xr.at[s, hi, t], x_sem.at[(s * nh + hi) * halves + t],
+                    device(d, m, hh * CORES + lo),
+                )
     keep_act = pltpu.make_async_copy(act, act_out, out_sem.at[1])
     keep_act.start()
 
     lane = lax.broadcasted_iota(jnp.int32, (tokens, LANES), 1)
-    for s in range(dp):
-        for hh in others_hi:
-            arrived(xr.at[s, hh], x_sem.at[s * nh + hh])
+
+    def combine(s):
         squares = jnp.zeros((tokens, 1), F32)
         along = jnp.zeros((tokens, 1), F32)
+        per = TILE // chunk
         for k in range(half // chunk):
             block = lo * (half // chunk) + k
             c = k * chunk
-            branch = xr[s, 0, :, c:c + chunk].astype(F32)
+            t, inner = k // per, slice(k % per * chunk, (k % per + 1) * chunk)
+            if k % per == 0:
+                for hh in others_hi:
+                    arrived(xr.at[s, hh, t], x_sem.at[(s * nh + hh) * halves + t])
+            branch = xr[s, 0, t, :, inner].astype(F32)
             for hh in range(1, nh):
-                branch = branch + xr[s, hh, :, c:c + chunk].astype(F32)
+                branch = branch + xr[s, hh, t, :, inner].astype(F32)
             comb = h[block % mp, block // mp, s].astype(F32) + branch
             bp[s, :, c:c + chunk] = comb
             cs[s, :, c:c + chunk] = comb.astype(BF16)
@@ -250,9 +291,7 @@
             ).start()
         push(cs.at[s], cr.at[s], c_sem.at[s], device(d, m, sib))
 
-    for dd in others_d:
-        arrived(pool.at[dd], pool_sem.at[dd])
-    for s in range(dp):
+    def slopes_of(s):
         arrived(sc.at[s], sc_recv.at[s])
         pooled = pool[s, 0]
 
@@ -292,13 +331,18 @@
                 cols = pl.ds(pl.multiple_of(base + c, TILE), TILE)
                 sf[s, :, cols] = slope
                 sh[s, :, cols] = slope.astype(BF16)
-        for c in range(0, ff, TILE):
-            term = dot_nt(sh[s], wout[c:c + TILE, :])
-            bk[s, :, c:c + TILE] = term
-            ks[s, :, c:c + TILE] = term.astype(BF16)
-        for slot, dd in enumerate(others_d):
-            slot = dp - 2 - slot
-            push(ks.at[s], gr.at[s, slot], k_sem.at[s * dp + slot], device(dd, m, p))
+        for t in range(tiles):
+            cols = slice(t * TILE, (t + 1) * TILE)
+            term = dot_nt(sh[s], wout[cols, :])
+            bk[s, :, cols] = term
+            ks[s, t] = term.astype(BF16)
+            send_tile(ks, s, t, k_sem)
+
+    for dd in others_d:
+        arrived(pool.at[dd], pool_sem.at[dd])
+    for s in range(dp):
+        combine(s)
+        slopes_of(s)
     keep_sh = pltpu.make_async_copy(sh, sh_out, out_sem.at[2])
     keep_sh.start()
     spot = lax.broadcasted_iota(jnp.int32, (8, LANES), 1)
@@ -307,76 +351,50 @@
     pen_out[...] = flat[:, :seqs]
 
     for s in range(dp):
-        for slot in range(dp - 1):
-            arrived(gr.at[s, slot], k_sem.at[s * dp + slot])
-        for c in range(0, ff, TILE):
-            raw = bk[s, :, c:c + TILE]
+        for t in range(tiles):
+            cols = slice(t * TILE, (t + 1) * TILE)
+            raw = bk[s, :, cols]
             for slot in range(dp - 1):
-                raw = raw + gr[s, slot, :, c:c + TILE].astype(F32)
-            gate = gp[s, :, c:c + TILE]
+                arrived(gr.at[s, slot, t], tile_sem(k_sem, s, slot, t))
+                raw = raw + gr[s, slot, t].astype(F32)
+            gate = gp[s, :, cols]
             sig = sigmoid(gate)
-            bg[s, :, c:c + TILE] = (raw * (sig * (1.0 + gate * (1.0 - sig)))).astype(BF16)
+            bg[s, :, cols] = (raw * (sig * (1.0 + gate * (1.0 - sig)))).astype(BF16)
 
         def hidden_term(hh, j, cc):
             first = (j * mp + hh * CORES + cc) * chunk
             return dot_nt(bg[s], win[pl.ds(pl.multiple_of(first, chunk), chunk), :])
 
-        for hh in range(nh):
+        for hh in others_hi + [hi]:
             for j in range(mloc):
                 fs[s, hh, j] = hidden_term(hh, j, 1 - lo).astype(BF16)
-        push(fs.at[s], fr.at[s], f_sem.at[s], device(d, m, sib))
-        for hh in range(nh):
+            push(fs.at[s, hh], fr.at[s, hh], f_sem.at[s * nh + hh], device(d, m, sib))
             for j in range(mloc):
                 fo[s, hh, j] = hidden_term(hh, j, lo)
-        arrived(fr.at[s], f_sem.at[s])
-        for hh in others_hi:
+            if hh is hi:
+                continue
+            arrived(fr.at[s, hh], f_sem.at[s * nh + hh])
             x2s[s, hh] = (fo[s, hh] + fr[s, hh].astype(F32)).astype(BF16)
             push(x2s.at[s, hh], x2r.at[s, hi], x2_sem.at[s * nh + hi], device(d, m, hh * CORES + lo))
     keep_bg = pltpu.make_async_copy(bg, bg_out, out_sem.at[3])
     keep_bg.start()
 
-    last = []
     for s in range(dp):
+        arrived(fr.at[s, hi], f_sem.at[s * nh + hi])
         for hh in others_hi:
             arrived(x2r.at[s, hh], x2_sem.at[s * nh + hh])
-        for j in range(mloc):
-            total = fo[s, hi, j] + fr[s, hi, j].astype(F32)
-            for hh in others_hi:
-                total = total + x2r[s, hh, j].astype(F32)
-            cols = pl.ds(pl.multiple_of((j * mp + p) * chunk, chunk), chunk)
-            ts[s, j] = (total + sf[s, :, cols]).astype(BF16)
-            to = d * mloc + j
-            here = jnp.logical_and(d == s, to == m)
-            away = pltpu.make_async_remote_copy(
-                src_ref=ts.at[s, j], dst_ref=zr.at[m],
-                send_sem=t_send.at[s * mloc + j], recv_sem=t_recv.at[m],
-                device_id=device(jnp.int32(s), to, p), device_id_type=MESH,
-            )
-            near = pltpu.make_async_copy(ts.at[s, j], zr.at[m], t_recv.at[m])
-
-            @pl.when(here)
-            def _(near=near):
-                near.start()
-
-            @pl.when(jnp.logical_not(here))
-            def _(away=away):
-                away.start()
-
-            last.append((here, away))
-
-    arrived(zr.at[0], t_recv.at[0])
-    total = zr[0].astype(F32)
-    for mm in range(1, members):
-        arrived(zr.at[mm], t_recv.at[mm])
-        total = total + zr[mm].astype(F32)
-    gh_out[...] = total
+    for k, out in enumerate(chunk_outs):
+        n = lax.rem(m + k, members)
+        s, j = n // mloc, lax.rem(n, mloc)
+        total = fo[s, hi, j] + fr[s, hi, j].astype(F32)
+        for hh in others_hi:
+            total = total + x2r[s, hh, j].astype(F32)
+        cols = pl.ds(pl.multiple_of((j * mp + p) * chunk, chunk), chunk)
+        out[...] = (total + sf[s, :, cols]).astype(BF16)
 
     for copy in sent:
-        copy.wait_send()
-    for here, away in last:
-        @pl.when(jnp.logical_not(here))
-        def _(away=away):
-            away.wait_send()
+        if all(copy is not done for done in waited):
+            copy.wait_send()
     for s in range(dp):
         some = sc.at[s, pl.ds(0, len(group))]
         pltpu.make_async_copy(some, some, sc_send.at[s]).wait()
@@ -384,7 +402,7 @@
         copy.wait()
 
 
-def weight_kernel(slabs, h_ref, bg_ref, act_ref, sh_ref, gin_ref, gout_ref):
+def weight_kernel(slabs, h_ref, bg_ref, act_ref, sh_ref, pen_ref, gin_ref, gout_ref, pen_out):
     def terms(left, right):
         total = None
         for s in range(slabs):
@@ -393,6 +411,7 @@
             total = term if total is None else total + term
         return total
 
+    pen_out[...] = pen_ref[...]
     gin_ref[0] = terms(lambda s: h_ref[0, 0, s], bg_ref)
     gout_ref[0] = terms(lambda s: act_ref[s], sh_ref)
 
@@ -416,19 +435,19 @@
         V = pltpu.VMEM
         dma = lambda n: pltpu.SemaphoreType.DMA((n,))
         sds = jax.ShapeDtypeStruct
+        sends = 64 + 16 * dp + 2 * dp * dp * (ff // TILE)
         flops = 8 * dp * tokens * rows * ff
-        pen, gh, h, act, sh, bg = pl.pallas_call(
+        pen, h, act, sh, bg, *chunks = pl.pallas_call(
             functools.partial(trunk_kernel, sizes),
             out_shape=(
                 sds((1, seqs), F32),
-                sds((tokens, chunk), F32),
                 sds((mp, mloc, dp, tokens, chunk), BF16),
                 sds((dp, tokens, ff), BF16),
                 sds((dp, tokens, rows), BF16),
                 sds((dp, tokens, ff), BF16),
-            ),
+            ) + (sds((tokens, chunk), BF16),) * members,
             in_specs=[smem, smem, smem, hbm, vmem, hbm, hbm],
-            out_specs=(vmem, vmem, hbm, hbm, hbm, hbm),
+            out_specs=(vmem, hbm, hbm, hbm, hbm) + (vmem,) * members,
             scratch_shapes=[
                 V((rows, ff), BF16),
                 V((ff, rows), BF16),
@@ -436,13 +455,13 @@
                 V((mp, mloc, dp, tokens, chunk), BF16),
                 V((dp, 2, 8, tokens), F32),
                 V((dp, tokens, ff), F32),
-                V((dp, tokens, ff), BF16),
-                V((dp, dp - 1, tokens, ff), BF16),
+                V((dp, ff // TILE, tokens, TILE), BF16),
+                V((dp, dp - 1, ff // TILE, tokens, TILE), BF16),
                 V((dp, tokens, ff), BF16),
                 V((dp, tokens, half), F32),
-                V((dp, tokens, half), BF16),
-                V((dp, tokens, half), BF16),
-                V((dp, nh, tokens, half), BF16),
+                V((dp, half // TILE, tokens, TILE), BF16),
+                V((dp, half // TILE, tokens, TILE), BF16),
+                V((dp, nh, half // TILE, tokens, TILE), BF16),
                 V((dp, tokens, half), BF16),
                 V((dp, tokens, half), BF16),
                 V((dp, 8, tokens), F32),
@@ -451,18 +470,17 @@
                 V((dp, tokens, rows), F32),
                 V((dp, tokens, rows), BF16),
                 V((dp, tokens, ff), F32),
-                V((dp, tokens, ff), BF16),
+                V((dp, ff // TILE, tokens, TILE), BF16),
                 V((dp, tokens, ff), BF16),
                 V((dp, nh, mloc, tokens, chunk), BF16),
                 V((dp, nh, mloc, tokens, chunk), BF16),
                 V((dp, nh, mloc, tokens, chunk), F32),
                 V((dp, nh, mloc, tokens, chunk), BF16),
                 V((dp, nh, mloc, tokens, chunk), BF16),
-                V((dp, mloc, tokens, chunk), BF16),
-                V((members, tokens, chunk), BF16),
-                dma(2), dma(4), dma(128), dma(members), dma(mp * mloc * dp), dma(dp),
-                dma(dp * dp), dma(dp), dma(dp * nh), dma(dp), dma(dp), dma(dp),
-                dma(dp * dp), dma(dp), dma(dp * nh), dma(dp * mloc), dma(members),
+                dma(2), dma(4), dma(sends), dma(members), dma(mp * mloc * dp), dma(dp),
+                dma(dp * dp * (ff // TILE)), dma(dp * (half // TILE)),
+                dma(dp * nh * (half // TILE)), dma(dp), dma(dp), dma(dp),
+                dma(dp * dp * (ff // TILE)), dma(dp * nh), dma(dp * nh),
             ],
             compiler_params=pltpu.CompilerParams(
                 collective_id=0, has_side_effects=True, vmem_limit_bytes=60 * 2**20
@@ -475,25 +493,39 @@
         steps = mloc * mp
         out_rows = ff // steps
         whole = lambda *shape: pl.BlockSpec(shape, lambda i: (0,) * len(shape))
-        gin, gout = pl.pallas_call(
+        moved = []
+        for k in range(members):
+            pairs = []
+            for dd in range(dp):
+                for mm in range(members):
+                    n = (k + mm) % members
+                    to = (n // mloc) * members + dd * mloc + n % mloc
+                    pairs.append((dd * members + mm, to))
+            moved.append(lax.ppermute(chunks[k], ("dp", "member"), pairs))
+        gin, gout, pen = pl.pallas_call(
             functools.partial(weight_kernel, dp),
             grid=(steps,),
-            out_shape=(sds((1, rows, ff), F32), sds((1, ff, rows), F32)),
+            out_shape=(sds((1, rows, ff), F32), sds((1, ff, rows), F32), sds((1, seqs), F32)),
             in_specs=[
                 pl.BlockSpec((1, 1, dp, tokens, chunk), lambda i: (i % mp, i // mp, 0, 0, 0)),
                 whole(dp, tokens, ff),
                 pl.BlockSpec((dp, tokens, out_rows), lambda i: (0, 0, i)),
                 whole(dp, tokens, rows),
+                whole(1, seqs),
             ],
             out_specs=(
                 pl.BlockSpec((1, chunk, ff), lambda i: (0, i, 0)),
                 pl.BlockSpec((1, out_rows, rows), lambda i: (0, i, 0)),
+                whole(1, seqs),
             ),
-            compiler_params=pltpu.CompilerParams(vmem_limit_bytes=40 * 2**20),
+            compiler_params=pltpu.CompilerParams(vmem_limit_bytes=60 * 2**20),
             cost_estimate=pl.CostEstimate(
                 flops=flops // 2, bytes_accessed=8 * rows * ff, transcendentals=0
             ),
-        )(h, bg, act, sh)
+        )(h, bg, act, sh, pen)
+        gh = moved[0].astype(F32)
+        for part in moved[1:]:
+            gh = gh + part.astype(F32)
         return pen, gh, gin, gout
 
     in_specs = (

time: 92 us -> 91.4 us (level)
  the two profiles are of different devices: /device:TPU:13 before, /device:TPU:0 now
where the time goes in v2:
time: 91.4 us; the launch traced here: 90.9 us
  Pallas kernels  81.4 us (89%)
  starting transfers between devices  8.13 us (9%)
    pallas_call x1, Pallas kernels, local(): pl.pallas_call(functools.partial(trunk_kernel, sizes), out_shape=(sds((1,...  71.4 us
    pallas_call x1, Pallas kernels, local(): pl.pallas_call(functools.partial(weight_kernel, dp), grid=(steps,), out_s...  10 us
    ppermute x4, starting transfers between devices, local(): moved.append(lax.ppermute(chunks[k], ('dp', 'member'), pairs))  8.13 us
  transfers between devices with their start and end apart: 4, of which 0 were waited for; matrix products, arithmetic and copies ran while one was open for 0% of the time, Pallas kernels for 11%

profile of v2, /device:TPU:0, one launch (start us, length us, event | category | flops | bytes accessed | tf_op | source)
XLA Modules:
  0.0 90.9 jit_solution(1007383301791509001)
XLA Ops:
  0.6 71.4 %shard_map.102 = (f32[1,4]{1,0:T(1,128)}, bf16[4,2,2,128,256]{4,3,2,1,0:T(8,128)(2,1)}, bf16[2,128,1024]{2,1,0:T(8,128)(2,1)}, bf16[2,128,2048]{2,1,0:T(8,128)(2...) custom-call(s32[1,4]{1,0:T(1,128)} %len_ref.1, ...), custom_call_target="tpu_custom_call" | custom-call | flops 4294967296 | bytes 8388608 | tf_op jit(solution)/shard_map/pallas_call | solution.py:440
  72.1 1.5 %collective-permute-start = (bf16[128,256]{1,0:T(8,128)(2,1)}, bf16[128,256]{1,0:T(8,128)(2,1)S(1)}, u32[]{:S(2)}, u32[]{:S(2)}) collective-permute-start(bf16[128,256]{1,0:T(8,128)(2,1)} %get-tuple-element.22), channel_id=1, source_target_pairs={{0,0},{4,4},{8,16},{12,20},{16,8},{20,12},{24,24},{28,28},{1,1},{5... | collective-permute-start | bytes 196616 | tf_op jit(solution)/shard_map/ppermute | solution.py:504
  73.6 0.7 collective-permute-start.1
  74.2 4.4 %collective-permute-start.2 = (bf16[128,256]{1,0:T(8,128)(2,1)}, bf16[128,256]{1,0:T(8,128)(2,1)S(1)}, u32[]{:S(2)}, u32[]{:S(2)}) collective-permute-start(bf16[128,256]{1,0:T(8,128)(2,1)} %get-tuple-element.24), channel_id=1, source_target_pairs={{0,16},{4,20},{8,0},{12,4},{16,24},{20,28},{24,8},{28,12},{1,17},{... | collective-permute-start | bytes 196616 | tf_op jit(solution)/shard_map/ppermute | solution.py:504
  78.6 1.5 %collective-permute-start.3 = (bf16[128,256]{1,0:T(8,128)(2,1)}, bf16[128,256]{1,0:T(8,128)(2,1)S(1)}, u32[]{:S(2)}, u32[]{:S(2)}) collective-permute-start(bf16[128,256]{1,0:T(8,128)(2,1)} %get-tuple-element.25), channel_id=1, source_target_pairs={{0,20},{4,0},{8,4},{12,16},{16,28},{20,8},{24,12},{28,24},{1,21},{... | collective-permute-start | bytes 196616 | tf_op jit(solution)/shard_map/ppermute | solution.py:504
  80.2 10.0 %shard_map.103 = (f32[1,2048,1024]{2,1,0:T(8,128)}, f32[1,1024,2048]{2,1,0:T(8,128)}, f32[1,4]{1,0:T(1,128)}) custom-call(bf16[4,2,2,128,256]{4,3,2,1,0:T(8,128)(2,1)} %get-tuple-element.16.h_ref, bf16[2,128,1024]{2,1,0:T(8,128)(2,1)} %get-tuple-element.17.bg_ref, bf16[2,128,1024]{2,1,0:T(8,128)(2,1)} %get-tuple-element.18.act_ref, ...), custom_call_target="tpu_custom_call" | custom-call | flops 2147483648 | bytes 16777216 | tf_op jit(solution)/shard_map/pallas_call | solution.py:505
  90.2 0.0 collective-permute-done
  90.2 0.0 collective-permute-done.1
  90.2 0.0 collective-permute-done.2
  90.2 0.0 collective-permute-done.3
  90.2 0.7 convert_add_fusion
Async XLA Ops:
  72.1 18.2 %collective-permute-start = (bf16[128,256]{1,0:T(8,128)(2,1)}, bf16[128,256]{1,0:T(8,128)(2,1)S(1)}, u32[]{:S(2)}, u32[]{:S(2)}) collective-permute-start(bf16[128,256]{1,0:T(8,128)(2,1)} %get-tuple-element.22), channel_id=1, source_target_pairs={{0,0},{4,4},{8,16},{12,20},{16,8},{20,12},{24,24},{28,28},{1,1},{5... | collective-permute-start | bytes 196616 | tf_op jit(solution)/shard_map/ppermute | solution.py:504
  73.6 16.7 %collective-permute-start.1 = (bf16[128,256]{1,0:T(8,128)(2,1)}, bf16[128,256]{1,0:T(8,128)(2,1)S(1)}, u32[]{:S(2)}, u32[]{:S(2)}) collective-permute-start(bf16[128,256]{1,0:T(8,128)(2,1)} %get-tuple-element.23), channel_id=1, source_target_pairs={{0,4},{4,16},{8,20},{12,0},{16,12},{20,24},{24,28},{28,8},{1,5},{5... | collective-permute-start | bytes 196616 | tf_op jit(solution)/shard_map/ppermute | solution.py:504
  74.2 16.0 %collective-permute-start.2 = (bf16[128,256]{1,0:T(8,128)(2,1)}, bf16[128,256]{1,0:T(8,128)(2,1)S(1)}, u32[]{:S(2)}, u32[]{:S(2)}) collective-permute-start(bf16[128,256]{1,0:T(8,128)(2,1)} %get-tuple-element.24), channel_id=1, source_target_pairs={{0,16},{4,20},{8,0},{12,4},{16,24},{20,28},{24,8},{28,12},{1,17},{... | collective-permute-start | bytes 196616 | tf_op jit(solution)/shard_map/ppermute | solution.py:504
  78.6 11.6 %collective-permute-start.3 = (bf16[128,256]{1,0:T(8,128)(2,1)}, bf16[128,256]{1,0:T(8,128)(2,1)S(1)}, u32[]{:S(2)}, u32[]{:S(2)}) collective-permute-start(bf16[128,256]{1,0:T(8,128)(2,1)} %get-tuple-element.25), channel_id=1, source_target_pairs={{0,20},{4,0},{8,4},{12,16},{16,28},{20,8},{24,12},{28,24},{1,21},{... | collective-permute-start | bytes 196616 | tf_op jit(solution)/shard_map/ppermute | solution.py:504

commit v3 on v2

--- a/solution.py
+++ b/solution.py
@@ -35,25 +35,11 @@
 def trunk_kernel(
     sizes,
     len_ref, off_ref, sw_ref, hid_ref, vec_ref, win_hbm, wout_hbm,
-    *rest,
-):
-    members = sizes[1]
-    pen_out, h_out, act_out, sh_out, bg_out = rest[:5]
-    chunk_outs = rest[5:5 + members]
-    trunk_body(
-        sizes, len_ref, off_ref, sw_ref, hid_ref, vec_ref, win_hbm, wout_hbm,
-        pen_out, h_out, act_out, sh_out, bg_out, chunk_outs, *rest[5 + members:]
-    )
-
-
-def trunk_body(
-    sizes,
-    len_ref, off_ref, sw_ref, hid_ref, vec_ref, win_hbm, wout_hbm,
-    pen_out, h_out, act_out, sh_out, bg_out, chunk_outs,
+    pen_out, gh_out, h_out, act_out, sh_out, bg_out,
     win, wout, z, h, pool, gp, gs, gr, act, bp, bs, br, xr, cs, cr, ps, sc, pens,
-    sf, sh, bk, ks, bg, fs, fr, fo, x2s, x2r,
+    sf, sh, bk, ks, bg, fs, fr, fo, x2s, x2r, ts, zr,
     local_sem, out_sem, send_sem, z_sem, h_sem, pool_sem, g_sem, b_sem, x_sem, c_sem,
-    sc_send, sc_recv, k_sem, f_sem, x2_sem,
+    sc_send, sc_recv, k_sem, f_sem, x2_sem, t_send, t_recv,
 ):
     dp, members, mp, tokens, chunk, ff, seqs, features = sizes
     nh = mp // CORES
@@ -74,12 +60,13 @@
 
     sent = []
 
-    def push(src, dst, sem, to):
+    def push(src, dst, sem, to, now=True):
         copy = pltpu.make_async_remote_copy(
             src_ref=src, dst_ref=dst, send_sem=send_sem.at[len(sent)], recv_sem=sem,
             device_id=to, device_id_type=MESH,
         )
-        copy.start()
+        if now:
+            copy.start()
         sent.append(copy)
         return copy
 
@@ -139,18 +126,38 @@
     for dd in others_d:
         push(pool.at[d], pool.at[d], pool_sem.at[d], device(dd, m, p))
 
+    across, along_mp = [], []
     for dd in others_d:
         for j in range(mloc):
             c = dd * mloc + j
-            arrived(z.at[c], z_sem.at[c])
-            push(z.at[c], h.at[p, j, d], hsem(p, j, d), device(dd, m, p))
+            across.append((c, [push(
+                z.at[c], h.at[p, j, d], hsem(p, j, d), device(dd, m, p), False
+            )]))
     for j in range(mloc):
         c = d * mloc + j
-        arrived(z.at[c], z_sem.at[c])
-        for hh in others_hi:
-            push(z.at[c], h.at[p, j, d], hsem(p, j, d), device(d, m, hh * CORES + lo))
-        push(z.at[c], h.at[p, j, d], hsem(p, j, d), device(d, m, sib))
-        pltpu.make_async_copy(z.at[c], h.at[p, j, d], hsem(p, j, d)).start()
+        copies = [
+            push(z.at[c], h.at[p, j, d], hsem(p, j, d), device(d, m, to), False)
+            for to in [hh * CORES + lo for hh in others_hi] + [sib]
+        ]
+        copies.append(pltpu.make_async_copy(z.at[c], h.at[p, j, d], hsem(p, j, d)))
+        along_mp.append((c, copies))
+
+    def forward(entries):
+        for c, copies in entries:
+            arrived(z.at[c], z_sem.at[c])
+            for copy in copies:
+                copy.start()
+
+    near_own = m // mloc == d
+
+    @pl.when(near_own)
+    def _():
+        forward(along_mp + across)
+
+    @pl.when(jnp.logical_not(near_own))
+    def _():
+        forward(across + along_mp)
+
     for dd in others_d:
         for j in range(mloc):
             arrived(h.at[p, j, dd], hsem(p, j, dd))
@@ -350,6 +357,37 @@
     flat = jnp.sum(jnp.where(diag, pens[d], 0.0), axis=0, keepdims=True)
     pen_out[...] = flat[:, :seqs]
 
+    last = []
+
+    def finish(s):
+        arrived(fr.at[s, hi], f_sem.at[s * nh + hi])
+        for hh in others_hi:
+            arrived(x2r.at[s, hh], x2_sem.at[s * nh + hh])
+        for j in range(mloc):
+            total = fo[s, hi, j] + fr[s, hi, j].astype(F32)
+            for hh in others_hi:
+                total = total + x2r[s, hh, j].astype(F32)
+            cols = pl.ds(pl.multiple_of((j * mp + p) * chunk, chunk), chunk)
+            ts[s, j] = (total + sf[s, :, cols]).astype(BF16)
+            to = d * mloc + j
+            here = jnp.logical_and(d == s, to == m)
+            away = pltpu.make_async_remote_copy(
+                src_ref=ts.at[s, j], dst_ref=zr.at[m],
+                send_sem=t_send.at[s * mloc + j], recv_sem=t_recv.at[m],
+                device_id=device(jnp.int32(s), to, p), device_id_type=MESH,
+            )
+            near = pltpu.make_async_copy(ts.at[s, j], zr.at[m], t_recv.at[m])
+
+            @pl.when(here)
+            def _(near=near):
+                near.start()
+
+            @pl.when(jnp.logical_not(here))
+            def _(away=away):
+                away.start()
+
+            last.append((here, away))
+
     for s in range(dp):
         for t in range(tiles):
             cols = slice(t * TILE, (t + 1) * TILE)
@@ -376,25 +414,26 @@
             arrived(fr.at[s, hh], f_sem.at[s * nh + hh])
             x2s[s, hh] = (fo[s, hh] + fr[s, hh].astype(F32)).astype(BF16)
             push(x2s.at[s, hh], x2r.at[s, hi], x2_sem.at[s * nh + hi], device(d, m, hh * CORES + lo))
+        if s > 0:
+            finish(s - 1)
     keep_bg = pltpu.make_async_copy(bg, bg_out, out_sem.at[3])
     keep_bg.start()
-
-    for s in range(dp):
-        arrived(fr.at[s, hi], f_sem.at[s * nh + hi])
-        for hh in others_hi:
-            arrived(x2r.at[s, hh], x2_sem.at[s * nh + hh])
-    for k, out in enumerate(chunk_outs):
-        n = lax.rem(m + k, members)
-        s, j = n // mloc, lax.rem(n, mloc)
-        total = fo[s, hi, j] + fr[s, hi, j].astype(F32)
-        for hh in others_hi:
-            total = total + x2r[s, hh, j].astype(F32)
-        cols = pl.ds(pl.multiple_of((j * mp + p) * chunk, chunk), chunk)
-        out[...] = (total + sf[s, :, cols]).astype(BF16)
+    finish(dp - 1)
+
+    for mm in range(members):
+        arrived(zr.at[mm], t_recv.at[mm])
+    total = zr[0].astype(F32)
+    for mm in range(1, members):
+        total = total + zr[mm].astype(F32)
+    gh_out[...] = total
 
     for copy in sent:
         if all(copy is not done for done in waited):
             copy.wait_send()
+    for here, away in last:
+        @pl.when(jnp.logical_not(here))
+        def _(away=away):
+            away.wait_send()
     for s in range(dp):
         some = sc.at[s, pl.ds(0, len(group))]
         pltpu.make_async_copy(some, some, sc_send.at[s]).wait()
@@ -402,18 +441,21 @@
         copy.wait()
 
 
-def weight_kernel(slabs, h_ref, bg_ref, act_ref, sh_ref, pen_ref, gin_ref, gout_ref, pen_out):
-    def terms(left, right):
-        total = None
-        for s in range(slabs):
-            term = lax.dot_general(left(s), right[s], ALONG, preferred_element_type=F32)
-            term = term.astype(BF16).astype(F32)
-            total = term if total is None else total + term
-        return total
-
+def weight_kernel(
+    h_ref, bg_ref, act_ref, sh_ref, pen_ref, gh_ref, gin_ref, gout_ref, pen_out, gh_out
+):
     pen_out[...] = pen_ref[...]
-    gin_ref[0] = terms(lambda s: h_ref[0, 0, s], bg_ref)
-    gout_ref[0] = terms(lambda s: act_ref[s], sh_ref)
+    gh_out[...] = gh_ref[...]
+
+    def flat(ref):
+        value = ref[...]
+        return value.reshape(value.shape[-3] * value.shape[-2], value.shape[-1])
+
+    def product(left, right):
+        return lax.dot_general(left, right, ALONG, preferred_element_type=F32)
+
+    gin_ref[0] = product(flat(h_ref), flat(bg_ref))
+    gout_ref[0] = product(flat(act_ref), flat(sh_ref))
 
 
 def solution(mesh):
@@ -437,17 +479,18 @@
         sds = jax.ShapeDtypeStruct
         sends = 64 + 16 * dp + 2 * dp * dp * (ff // TILE)
         flops = 8 * dp * tokens * rows * ff
-        pen, h, act, sh, bg, *chunks = pl.pallas_call(
+        pen, gh, h, act, sh, bg = pl.pallas_call(
             functools.partial(trunk_kernel, sizes),
             out_shape=(
                 sds((1, seqs), F32),
+                sds((tokens, chunk), F32),
                 sds((mp, mloc, dp, tokens, chunk), BF16),
                 sds((dp, tokens, ff), BF16),
                 sds((dp, tokens, rows), BF16),
                 sds((dp, tokens, ff), BF16),
-            ) + (sds((tokens, chunk), BF16),) * members,
+            ),
             in_specs=[smem, smem, smem, hbm, vmem, hbm, hbm],
-            out_specs=(vmem, hbm, hbm, hbm, hbm) + (vmem,) * members,
+            out_specs=(vmem, vmem, hbm, hbm, hbm, hbm),
             scratch_shapes=[
                 V((rows, ff), BF16),
                 V((ff, rows), BF16),
@@ -477,10 +520,13 @@
                 V((dp, nh, mloc, tokens, chunk), F32),
                 V((dp, nh, mloc, tokens, chunk), BF16),
                 V((dp, nh, mloc, tokens, chunk), BF16),
+                V((dp, mloc, tokens, chunk), BF16),
+                V((members, tokens, chunk), BF16),
                 dma(2), dma(4), dma(sends), dma(members), dma(mp * mloc * dp), dma(dp),
                 dma(dp * dp * (ff // TILE)), dma(dp * (half // TILE)),
                 dma(dp * nh * (half // TILE)), dma(dp), dma(dp), dma(dp),
                 dma(dp * dp * (ff // TILE)), dma(dp * nh), dma(dp * nh),
+                dma(dp * mloc), dma(members),
             ],
             compiler_params=pltpu.CompilerParams(
                 collective_id=0, has_side_effects=True, vmem_limit_bytes=60 * 2**20
@@ -493,39 +539,30 @@
         steps = mloc * mp
         out_rows = ff // steps
         whole = lambda *shape: pl.BlockSpec(shape, lambda i: (0,) * len(shape))
-        moved = []
-        for k in range(members):
-            pairs = []
-            for dd in range(dp):
-                for mm in range(members):
-                    n = (k + mm) % members
-                    to = (n // mloc) * members + dd * mloc + n % mloc
-                    pairs.append((dd * members + mm, to))
-            moved.append(lax.ppermute(chunks[k], ("dp", "member"), pairs))
-        gin, gout, pen = pl.pallas_call(
-            functools.partial(weight_kernel, dp),
+        gin, gout, pen, gh = pl.pallas_call(
+            weight_kernel,
             grid=(steps,),
-            out_shape=(sds((1, rows, ff), F32), sds((1, ff, rows), F32), sds((1, seqs), F32)),
+            out_shape=(sds((1, rows, ff), F32), sds((1, ff, rows), F32), sds((1, seqs), F32),
+                       sds((tokens, chunk), F32)),
             in_specs=[
                 pl.BlockSpec((1, 1, dp, tokens, chunk), lambda i: (i % mp, i // mp, 0, 0, 0)),
                 whole(dp, tokens, ff),
                 pl.BlockSpec((dp, tokens, out_rows), lambda i: (0, 0, i)),
                 whole(dp, tokens, rows),
                 whole(1, seqs),
+                whole(tokens, chunk),
             ],
             out_specs=(
                 pl.BlockSpec((1, chunk, ff), lambda i: (0, i, 0)),
                 pl.BlockSpec((1, out_rows, rows), lambda i: (0, i, 0)),
                 whole(1, seqs),
+                whole(tokens, chunk),
             ),
             compiler_params=pltpu.CompilerParams(vmem_limit_bytes=60 * 2**20),
             cost_estimate=pl.CostEstimate(
                 flops=flops // 2, bytes_accessed=8 * rows * ff, transcendentals=0
             ),
-        )(h, bg, act, sh, pen)
-        gh = moved[0].astype(F32)
-        for part in moved[1:]:
-            gh = gh + part.astype(F32)
+        )(h, bg, act, sh, pen, gh)
         return pen, gh, gin, gout
 
     in_specs = (

time: 91.4 us -> 88.5 us (0.968)
  the two profiles are of different devices: /device:TPU:0 before, /device:TPU:13 now
where the time goes in v3:
time: 88.5 us; the launch traced here: 88.1 us
  Pallas kernels  87.5 us (99%)
    pallas_call x1, Pallas kernels, local(): pl.pallas_call(functools.partial(trunk_kernel, sizes), out_shape=(sds((1,...  78 us
    pallas_call x1, Pallas kernels, local(): pl.pallas_call(weight_kernel, grid=(steps,), out_shape=(sds((1, rows, ff)...  9.44 us

profile of v3, /device:TPU:13, one launch (start us, length us, event | category | flops | bytes accessed | tf_op | source)
XLA Modules:
  0.0 88.1 jit_solution(14982854132768356233)
XLA Ops:
  0.6 78.0 %shard_map.102 = (f32[1,4]{1,0:T(1,128)}, f32[128,256]{1,0:T(8,128)}, bf16[4,2,2,128,256]{4,3,2,1,0:T(8,128)(2,1)}, bf16[2,128,1024]{2,1,0:T(8,128)(2,1)}, bf16[...) custom-call(s32[1,4]{1,0:T(1,128)} %len_ref.1, s32[1,4]{1,0:T(1,128)} %off_ref.1, f32[1,4]{1,0:T(1,128)} %sw_ref.1, ...), custom_call_target="tpu_custom_call" | custom-call | flops 4294967296 | bytes 8388608 | tf_op jit(solution)/shard_map/pallas_call | solution.py:482
  78.7 9.4 %shard_map.103 = (f32[1,2048,1024]{2,1,0:T(8,128)}, f32[1,1024,2048]{2,1,0:T(8,128)}, f32[1,4]{1,0:T(1,128)}, f32[128,256]{1,0:T(8,128)}) custom-call(bf16[4,2,2,128,256]{4,3,2,1,0:T(8,128)(2,1)} %get-tuple-element.14.h_ref, bf16[2,128,1024]{2,1,0:T(8,128)(2,1)} %get-tuple-element.15.bg_ref, bf16[2,128,1024]{2,1,0:T(8,128)(2,1)} %get-tuple-element.16.act_ref, ...), custom_call_target="tpu_custom_call" | custom-call | flops 2147483648 | bytes 16777216 | tf_op jit(solution)/shard_map/pallas_call | solution.py:542

commit v4 on v3

--- a/solution.py
+++ b/solution.py
@@ -11,7 +11,6 @@
 SPREAD_FLOOR = 0.25
 EPSILON = 1e-05
 MESH = pl.DeviceIdType.MESH
-AGAINST = (((1,), (1,)), ((), ()))
 ALONG = (((0,), (0,)), ((), ()))
 F32 = jnp.float32
 BF16 = jnp.bfloat16
@@ -24,10 +23,6 @@
     return jnp.dot(a, b, preferred_element_type=F32)
 
 
-def dot_nt(a, b):
-    return lax.dot_general(a, b, AGAINST, preferred_element_type=F32)
-
-
 def sigmoid(v):
     return 1.0 / (1.0 + jnp.exp(-v))
 
@@ -37,7 +32,7 @@
     len_ref, off_ref, sw_ref, hid_ref, vec_ref, win_hbm, wout_hbm,
     pen_out, gh_out, h_out, act_out, sh_out, bg_out,
     win, wout, z, h, pool, gp, gs, gr, act, bp, bs, br, xr, cs, cr, ps, sc, pens,
-    sf, sh, bk, ks, bg, fs, fr, fo, x2s, x2r, ts, zr,
+    sf, sh, bk, ks, bg, fs, fr, fo, x2s, x2r, ts, zr, win_t, wout_t,
     local_sem, out_sem, send_sem, z_sem, h_sem, pool_sem, g_sem, b_sem, x_sem, c_sem,
     sc_send, sc_recv, k_sem, f_sem, x2_sem, t_send, t_recv,
 ):
@@ -202,8 +197,14 @@
             ))
         return copies
 
+    def turn(src, dst):
+        for a in range(0, src.shape[0], TILE):
+            for b in range(0, src.shape[1], TILE):
+                dst[b:b + TILE, a:a + TILE] = jnp.transpose(src[a:a + TILE, b:b + TILE])
+
     load_in.wait()
     gate_add(p, True)
+    turn(win, win_t)
     all_here(sib)
     gate_add(sib, False)
     for hh in others_hi:
@@ -236,6 +237,7 @@
     keep_h.start()
 
     load_out.wait()
+    turn(wout, wout_t)
     halves = half // TILE
     for s in range(dp):
         for t in range(tiles):
@@ -340,7 +342,7 @@
                 sh[s, :, cols] = slope.astype(BF16)
         for t in range(tiles):
             cols = slice(t * TILE, (t + 1) * TILE)
-            term = dot_nt(sh[s], wout[cols, :])
+            term = dot(sh[s], wout_t[:, cols])
             bk[s, :, cols] = term
             ks[s, t] = term.astype(BF16)
             send_tile(ks, s, t, k_sem)
@@ -401,7 +403,7 @@
 
         def hidden_term(hh, j, cc):
             first = (j * mp + hh * CORES + cc) * chunk
-            return dot_nt(bg[s], win[pl.ds(pl.multiple_of(first, chunk), chunk), :])
+            return dot(bg[s], win_t[:, pl.ds(pl.multiple_of(first, chunk), chunk)])
 
         for hh in others_hi + [hi]:
             for j in range(mloc):
@@ -522,6 +524,8 @@
                 V((dp, nh, mloc, tokens, chunk), BF16),
                 V((dp, mloc, tokens, chunk), BF16),
                 V((members, tokens, chunk), BF16),
+                V((ff, rows), BF16),
+                V((rows, ff), BF16),
                 dma(2), dma(4), dma(sends), dma(members), dma(mp * mloc * dp), dma(dp),
                 dma(dp * dp * (ff // TILE)), dma(dp * (half // TILE)),
                 dma(dp * nh * (half // TILE)), dma(dp), dma(dp), dma(dp),

time: 88.5 us -> 88.3 us (level)
  no operation moved by 1% of the time
where the time goes in v4:
time: 88.3 us; the launch traced here: 87.9 us
  Pallas kernels  87.2 us (99%)
    pallas_call x1, Pallas kernels, local(): pl.pallas_call(functools.partial(trunk_kernel, sizes), out_shape=(sds((1,...  77.8 us
    pallas_call x1, Pallas kernels, local(): pl.pallas_call(weight_kernel, grid=(steps,), out_shape=(sds((1, rows, ff)...  9.44 us

profile of v4, /device:TPU:13, one launch (start us, length us, event | category | flops | bytes accessed | tf_op | source)
XLA Modules:
  0.0 87.9 jit_solution(6535811742448215412)
XLA Ops:
  0.6 77.8 %shard_map.102 = (f32[1,4]{1,0:T(1,128)}, f32[128,256]{1,0:T(8,128)}, bf16[4,2,2,128,256]{4,3,2,1,0:T(8,128)(2,1)}, bf16[2,128,1024]{2,1,0:T(8,128)(2,1)}, bf16[...) custom-call(s32[1,4]{1,0:T(1,128)} %len_ref.1, s32[1,4]{1,0:T(1,128)} %off_ref.1, f32[1,4]{1,0:T(1,128)} %sw_ref.1, ...), custom_call_target="tpu_custom_call" | custom-call | flops 4294967296 | bytes 8388608 | tf_op jit(solution)/shard_map/pallas_call | solution.py:484
  78.4 9.4 %shard_map.103 = (f32[1,2048,1024]{2,1,0:T(8,128)}, f32[1,1024,2048]{2,1,0:T(8,128)}, f32[1,4]{1,0:T(1,128)}, f32[128,256]{1,0:T(8,128)}) custom-call(bf16[4,2,2,128,256]{4,3,2,1,0:T(8,128)(2,1)} %get-tuple-element.14.h_ref, bf16[2,128,1024]{2,1,0:T(8,128)(2,1)} %get-tuple-element.15.bg_ref, bf16[2,128,1024]{2,1,0:T(8,128)(2,1)} %get-tuple-element.16.act_ref, ...), custom_call_target="tpu_custom_call" | custom-call | flops 2147483648 | bytes 16777216 | tf_op jit(solution)/shard_map/pallas_call | solution.py:546
